TPU v7x, 256 devices: a whole 4x4x8 slice. The times are simulated.
256 devices in a mesh: side: 2 (over core), grp: 8 (over x, z_hi), tp: 16 (over z_lo, y).
Axes of the slice: x: 4, y: 4, z: 8 (z_hi: 2, z_lo: 4; z = z_hi * 4 + z_lo), core: 2. Of those that a mesh axis runs over, the one named last changes fastest.
Arguments:
- tokens: bfloat16 [8192, 8192], P(('side', 'grp'), 'tp'), may hold values from -8 to 8
- norm_gain: bfloat16 [8192], P('tp'), may hold values from 0.25 to 1.75
- wq: bfloat16 [8192, 8192], P('side', 'tp'), may hold values from -1 to 1
- wk: bfloat16 [8192, 1024], P('side', 'tp'), may hold values from -1 to 1
- wv: bfloat16 [8192, 1024], P('side', 'tp'), may hold values from -0.0625 to 0.0625
- wo: bfloat16 [8192, 8192], P('tp', 'side'), may hold values from -0.0625 to 0.0625
- span_offsets: int32 [16], P(('side', 'grp')), may hold values from 0 to 32767
- shared_pages: int32 [16, 32], P(('side', 'grp')), may hold values 0 or 1
- page_owner: int32 [16, 32, 1], P(('side', 'grp')), may hold values from 0 to 7; in each aligned block of 32 rows (0 to 31, 32 to 63, ..., all dimensions but the last counted through in order) at most 6 rows name the same one
- page_ids: int32 [16, 32], P(('side', 'grp')), may hold values from 0 to 65535
Outputs:
- mixed: bfloat16 [8192, 8192], P(('side', 'grp'), 'tp')
- kv_pool: bfloat16 [768, 32768], P(('side', 'grp'), 'tp')
- pool_ids: int32 [768], P(('side', 'grp'))
Inputs may be any that keep to these rules, and one draw needn't show every extreme that they name: `page_owner`: within the pages of one prompt block, at most 6 pages name one owner, a bound that some block reaches.
All inputs are finite; a program needn't handle non-finite values. No bound on the sum of `shared_pages` on one device may be relied on, other than what follows from the above.
Results may differ from a plain program's by a relative error of at most 0.02.
Values may be sent and summed in bfloat16 or wider, within the bound.
A program may use at most 128 MiB of HBM per device.

v0:
```python
import jax
import jax.numpy as jnp
from jax import lax
from jax.sharding import PartitionSpec as P

KVH = 8
HD = 128
PAGE = 16


EPS = 1e-05


def partner(block, axis, apart):
    count = lax.axis_size(axis)
    route = []
    for low in range(count):
        high = low | 1 << apart
        if high != low and high < count:
            route += [(low, high), (high, low)]
    return lax.ppermute(block, axis, route)


def from_behind(value, axis, steps):
    count = lax.axis_size(axis)
    pairs = [(source, (source + steps) % count) for source in range(count)]
    return lax.ppermute(value, axis, pairs)


def rotary(values, positions):
    half = values.shape[-1] // 2
    freq = jnp.exp(
        -jnp.log(500000.0) * (2.0 * jnp.arange(half, dtype=jnp.float32)) / values.shape[-1]
    )
    angle = positions.astype(jnp.float32)[:, None] * freq[None, :]
    cosine = jnp.cos(angle)[:, None, :]
    sine = jnp.sin(angle)[:, None, :]
    first = values[..., :half]
    second = values[..., half:]
    return jnp.concatenate(
        [first * cosine - second * sine, second * cosine + first * sine], axis=-1
    )


def shards(tokens, norm_gain, wq, wk, wv, wo, span_offsets, shared_pages, page_owner, page_ids):
    whole, gain = (
        lax.all_gather(tokens, "tp", axis=1, tiled=True),
        lax.all_gather(norm_gain, "tp", axis=0, tiled=True),
    )
    count = whole.shape[0]
    xf = whole.astype(jnp.float32)
    normed = (
        xf * lax.rsqrt(jnp.mean(xf * xf, axis=-1, keepdims=True) + EPS) * gain.astype(jnp.float32)
    ).astype(jnp.bfloat16)
    qcols = wq.shape[1]
    kcols = wk.shape[1]
    pieces = (
        lax.all_gather(wq, "side", axis=0, tiled=True),
        lax.all_gather(wk, "side", axis=0, tiled=True),
        lax.all_gather(wv, "side", axis=0, tiled=True),
    )
    q_raw, k_raw, v_raw = tuple(
        (jnp.dot(normed, piece, preferred_element_type=jnp.float32) for piece in pieces)
    )
    positions = span_offsets[0] + jnp.arange(count, dtype=jnp.int32)
    tp_index = lax.axis_index("tp")
    sharing = lax.axis_size("tp") // KVH
    k_block = k_raw
    v_block = v_raw
    other_k = partner(k_block.astype(jnp.bfloat16), "tp", 0).astype(k_block.dtype)
    other_v = partner(v_block.astype(jnp.bfloat16), "tp", 0).astype(v_block.dtype)
    upper_half = tp_index // (1 << 0) % 2 == 1
    k_block = jnp.where(
        upper_half,
        jnp.concatenate([other_k, k_block], axis=1),
        jnp.concatenate([k_block, other_k], axis=1),
    )
    v_block = jnp.where(
        upper_half,
        jnp.concatenate([other_v, v_block], axis=1),
        jnp.concatenate([v_block, other_v], axis=1),
    )
    query = rotary(q_raw.reshape(count, qcols // HD, HD), positions).astype(jnp.bfloat16)
    keys = rotary(k_block.reshape(count, 1, HD), positions).astype(jnp.bfloat16).reshape(count, HD)
    values = v_block.astype(jnp.bfloat16)
    scores = jnp.einsum("qhd,kd->hqk", query, keys, preferred_element_type=jnp.float32) / jnp.sqrt(
        jnp.float32(HD)
    )
    causal = jnp.arange(count)[:, None] >= jnp.arange(count)[None, :]
    scores = jnp.where(causal[None], scores, -1e30)
    top = jnp.max(scores, axis=-1, keepdims=True)
    weights = jnp.exp(scores - top)
    probs = (weights / jnp.sum(weights, axis=-1, keepdims=True)).astype(jnp.bfloat16)
    context = (
        jnp.einsum("hqk,kd->qhd", probs, values, preferred_element_type=jnp.float32)
        .astype(jnp.bfloat16)
        .reshape(count, qcols)
    )
    terms = jnp.dot(
        context, lax.all_gather(wo, "side", axis=1, tiled=True), preferred_element_type=jnp.float32
    )
    attended = lax.psum_scatter(
        terms.astype(jnp.bfloat16), "tp", scatter_dimension=1, tiled=True
    ).astype(jnp.float32)
    mixed = (tokens.astype(jnp.float32) + attended).astype(jnp.bfloat16)
    pages_dev = count // PAGE
    groups = lax.axis_size("grp")
    cap = max(2, 3 * pages_dev // (2 * groups))
    within_head = tp_index % sharing * kcols
    k_own = lax.dynamic_slice_in_dim(keys, within_head, kcols, 1)
    v_own = lax.dynamic_slice_in_dim(values, within_head, kcols, 1)
    rows = jnp.stack(
        [k_own.reshape(pages_dev, PAGE, kcols), v_own.reshape(pages_dev, PAGE, kcols)], axis=2
    ).reshape(pages_dev, PAGE * 2 * kcols)
    live = 1 - shared_pages[0]
    owner = page_owner[0, :, 0]
    onehot = (owner[:, None] == jnp.arange(groups, dtype=jnp.int32)[None, :]).astype(
        jnp.int32
    ) * live[:, None]
    rank = jnp.sum(jnp.cumsum(onehot, axis=0) * onehot, axis=1) - 1
    slots_count = groups * cap
    select = (
        (owner * cap + rank)[None, :] == jnp.arange(slots_count, dtype=jnp.int32)[:, None]
    ) & (live[None, :] == 1)
    buffer = jnp.dot(select.astype(jnp.bfloat16), rows, preferred_element_type=jnp.float32).astype(
        jnp.bfloat16
    )
    id_buffer = jnp.sum(select.astype(jnp.int32) * (page_ids[0] + 1)[None, :], axis=1) - 1
    buffer, id_buffer = (
        buffer.reshape(slots_count // cap, cap, rows.shape[1]),
        id_buffer.reshape(slots_count // cap, cap),
    )
    moved = (
        lax.all_to_all(buffer, "grp", split_axis=0, concat_axis=0, tiled=True),
        lax.all_to_all(id_buffer, "grp", split_axis=0, concat_axis=0, tiled=True),
    )
    got_pages, got_ids = from_behind((moved[0], moved[1]), "side", 1)
    kv_pool = got_pages.reshape(groups * cap, rows.shape[1])
    pool_ids = got_ids.reshape(groups * cap)
    return (mixed, kv_pool, pool_ids)


def solution(mesh):
    in_specs = (
        P(("side", "grp"), "tp"),
        P("tp"),
        P("side", "tp"),
        P("side", "tp"),
        P("side", "tp"),
        P("tp", "side"),
        P(("side", "grp")),
        P(("side", "grp"), None),
        P(("side", "grp"), None, None),
        P(("side", "grp"), None),
    )
    out_specs = (P(("side", "grp"), "tp"), P(("side", "grp"), "tp"), P(("side", "grp")))
    return jax.shard_map(shards, mesh=mesh, in_specs=in_specs, out_specs=out_specs, check_vma=False)
```

profile of v0, /device:TPU:2, one launch (start us, length us, event | category | flops | bytes accessed | tf_op | source)
XLA Modules:
  0.0 334.4 jit_solution(3213588003750043940)
XLA Ops:
  7.2 0.7 all-gather.7.cloned.1.call-update
  8.0 0.7 all-gather.13.cloned.1.call-update
  8.7 0.7 all-gather.11.cloned.1.call-update
  10.0 0.5 all-gather.15.cloned.1.call-update
  10.6 44.0 %all-gather = bf16[16,1,512]{2,1,0:T(2,128)(2,1)S(1)} all-gather(bf16[1,1,512]{2,1,0:T(2,128)(2,1)S(1)} %reshape.285), channel_id=1, replica_groups=mesh['side'=2,'grp'=8,'tp'=16] {'tp'}, dimensions={0}, use_global_device_ids=true | all-gather | bytes 17408 | tf_op jit(solution)/shard_map/all_gather | solution.py:48
  55.4 1.0 multiply_cosine_fusion
  56.4 59.1 %all-gather.7.cloned.1.call-done = bf16[512,8192]{1,0:T(8,128)(2,1)} async-done(((bf16[512,512]{1,0:T(8,128)(2,1)}), bf16[512,8192]{1,0:T(8,128)(2,1)}) %all-gather.7.cloned.1.call-update) | async-done | bytes 8388624 | tf_op jit(solution)/shard_map/all_gather | solution.py:47
  115.5 5.1 %fusion.1 = f32[512]{0:T(512)S(1)} fusion(bf16[512,8192]{1,0:T(8,128)(2,1)} %all-gather.7.cloned.1.call-done), kind=kLoop, calls=%fused_computation.3 | loop fusion | flops 12582400 | bytes 8390656 | tf_op jit(solution)/shard_map/reduce_sum | solution.py:53
  120.6 18.6 %all-gather.13.cloned.1.call-done = bf16[8192,512]{1,0:T(8,128)(2,1)} async-done(((bf16[4096,512]{1,0:T(8,128)(2,1)}), bf16[8192,512]{1,0:T(8,128)(2,1)}) %all-gather.13.cloned.1.call-update) | async-done | bytes 8388624 | tf_op jit(solution)/shard_map/all_gather | solution.py:58
  139.2 11.3 %fusion.35 = f32[512,512]{0,1:T(8,128)S(1)} fusion(bf16[8192,512]{1,0:T(8,128)(2,1)} %all-gather.13.cloned.1.call-done, bf16[512,8192]{1,0:T(8,128)(2,1)} %all-gather.7.cloned.1.call-done, f32[8192]{0:T(1024)S(1)} %bitcast.55, f32[512]{0:T(512)S(1)} %add_rsqrt_fusion), kind=kOutput, calls=%fused_computation.69 | convolution fusion | flops 4311744512 | bytes 17860608 | tf_op jit(solution)/shard_map/dot_general | solution.py:63
  151.3 5.4 %all-gather.11.cloned.1.call-done = bf16[8192,64]{0,1:T(8,128)(2,1)} async-done(((bf16[4096,64]{0,1:T(8,128)(2,1)}), bf16[8192,64]{0,1:T(8,128)(2,1)}) %all-gather.11.cloned.1.call-update) | async-done | bytes 1048592 | tf_op jit(solution)/shard_map/all_gather | solution.py:59
  156.7 6.3 %fusion.42 = (bf16[512,64]{0,1:T(8,128)(2,1)S(1)}, f32[512,64]{0,1:T(8,128)S(1)}) fusion(bf16[8192,64]{0,1:T(8,128)(2,1)} %all-gather.11.cloned.1.call-done, bf16[512,8192]{1,0:T(8,128)(2,1)} %all-gather.7.cloned.1.call-done, f32[8192]{0:T(1024)S(1)} %bitcast.56, f32[512]{0:T(512)S(1)} %add_rsqrt_fusion), kind=kOutput, calls=%fused_computation.73 | convolution fusion | flops 553680896 | bytes 9668608 | tf_op jit(solution)/shard_map/dot_general | solution.py:63
  163.0 1.8 collective-permute-start.1
  164.8 9.3 %all-gather.9.cloned.1.call-done = bf16[8192,64]{0,1:T(8,128)(2,1)} async-done(((bf16[4096,64]{0,1:T(8,128)(2,1)}), bf16[8192,64]{0,1:T(8,128)(2,1)}) %all-gather.9.cloned.1.call-update) | async-done | bytes 1048592 | tf_op jit(solution)/shard_map/all_gather | solution.py:60
  174.0 6.3 %fusion.39 = bf16[512,64]{0,1:T(8,128)(2,1)S(1)} fusion(bf16[8192,64]{0,1:T(8,128)(2,1)} %all-gather.9.cloned.1.call-done, bf16[512,8192]{1,0:T(8,128)(2,1)} %all-gather.7.cloned.1.call-done, f32[8192]{0:T(1024)S(1)} %bitcast.57, f32[512]{0:T(512)S(1)} %add_rsqrt_fusion), kind=kOutput, calls=%fused_computation.71 | convolution fusion | flops 553648128 | bytes 9537536 | tf_op jit(solution)/shard_map/dot_general | solution.py:63
  180.4 1.6 collective-permute-start
  182.2 2.5 collective-permute-done
  184.8 0.6 fusion.20
  185.4 0.8 fusion.10
  186.2 2.1 fusion.43
  188.8 13.3 %all-gather.15.cloned.1.call-done = bf16[512,8192]{1,0:T(8,128)(2,1)} async-done(((bf16[512,4096]{1,0:T(8,128)(2,1)}), bf16[512,8192]{1,0:T(8,128)(2,1)}) %all-gather.15.cloned.1.call-update) | async-done | bytes 8388624 | tf_op jit(solution)/shard_map/all_gather | solution.py:100
  202.2 10.1 %convolution_convert_fusion = bf16[512,8192]{1,0:T(8,128)(2,1)} fusion(bf16[512,512]{0,1:T(8,128)(2,1)S(1)} %bitcast.51, bf16[512,8192]{1,0:T(8,128)(2,1)} %all-gather.15.cloned.1.call-done), kind=kOutput, calls=%fused_computation.6 | convolution fusion | flops 4299161600 | bytes 17301504 | tf_op jit(solution)/shard_map/dot_general | solution.py:99
  212.3 0.6 copy-done.3
  214.6 0.8 reshape.281
  215.4 10.0 %all-to-all-start = ((bf16[8,6,2048]{2,1,0:T(8,128)(2,1)}), bf16[8,6,2048]{2,1,0:T(8,128)(2,1)S(1)}, u32[]{:S(2)}, u32[]{:S(2)}) async-start(bf16[8,6,2048]{2,1,0:T(8,128)(2,1)} %reshape.281), calls=%async_computation.1 | async-start | bytes 524288 | tf_op jit(solution)/shard_map/all_to_all | solution.py:134
  225.5 13.5 %all-to-all-done = bf16[8,6,2048]{2,1,0:T(8,128)(2,1)S(1)} async-done(((bf16[8,6,2048]{2,1,0:T(8,128)(2,1)}), bf16[8,6,2048]{2,1,0:T(8,128)(2,1)S(1)}, u32[]{:S(2)}, u32[]{:S(2)}) %all-to-all-start) | async-done | bytes 196640 | tf_op jit(solution)/shard_map/all_to_all | solution.py:134
  239.1 13.6 %all_to_all.14 = s32[8,1,6]{2,1,0:T(1,128)S(1)} all-to-all(s32[8,1,6]{2,1,0:T(1,128)S(1)} %bitcast.58), channel_id=1, replica_groups=mesh['side'=2,'grp'=8,'tp'=16] {'grp'}, dimensions={0} | all-to-all | bytes 384 | tf_op jit(solution)/shard_map/all_to_all | solution.py:135
  252.7 1.2 collective-permute-done.3
  253.9 0.6 reshape.283
  254.5 0.7 reshape.282
  255.2 70.3 %reduce-scatter.2.cloned.1.call-done = bf16[512,512]{1,0:T(8,128)(2,1)} async-done(((bf16[512,8192]{1,0:T(8,128)(2,1)}), bf16[512,512]{1,0:T(8,128)(2,1)}) %reduce-scatter.2.cloned.1.call-update) | async-done | bytes 524304 | tf_op jit(solution)/shard_map/reduce_scatter | solution.py:102
  325.6 2.0 add_convert_fusion
  (53 shorter events, 4.3 us)
Async XLA Ops:
  7.2 3.4 %copy-start.2 = (bf16[512]{0:T(512)(128)(2,1)S(1)}, bf16[512]{0:T(512)(128)(2,1)}, u32[]{:S(2)}) copy-start(bf16[512]{0:T(512)(128)(2,1)} %param.11) | copy-start | bytes 3076
  7.2 108.3 %all-gather.7.cloned.1.call-start = ((), (), s32[]{:S(2)}) async-start(), calls=%async_computation.3 | async-start | bytes 8912896 | tf_op jit(solution)/shard_map/all_gather | solution.py:47
  7.9 131.3 %all-gather.13.cloned.1.call-start = ((), (), s32[]{:S(2)}) async-start(), calls=%async_computation.6 | async-start | bytes 12582912 | tf_op jit(solution)/shard_map/all_gather | solution.py:58
  8.7 148.0 %all-gather.11.cloned.1.call-start = ((), (), s32[]{:S(2)}) async-start(), calls=%async_computation.5 | async-start | bytes 1572864 | tf_op jit(solution)/shard_map/all_gather | solution.py:59
  9.4 164.6 %all-gather.9.cloned.1.call-start = ((), (), s32[]{:S(2)}) async-start(), calls=%async_computation.4 | async-start | bytes 1572864 | tf_op jit(solution)/shard_map/all_gather | solution.py:60
  10.0 192.2 %all-gather.15.cloned.1.call-start = ((), (), s32[]{:S(2)}) async-start(), calls=%async_computation.7 | async-start | bytes 12582912 | tf_op jit(solution)/shard_map/all_gather | solution.py:100
  10.6 315.0 %reduce-scatter.2.cloned.1.call-start = ((), (), s32[]{:S(2)}) async-start(), calls=%async_computation.8 | async-start | bytes 8912896 | tf_op jit(solution)/shard_map/reduce_scatter | solution.py:102
  163.0 21.8 %collective-permute-start.1 = (bf16[512,64]{0,1:T(8,128)(2,1)S(1)}, bf16[512,64]{0,1:T(8,128)(2,1)S(1)}, u32[]{:S(2)}, u32[]{:S(2)}) collective-permute-start(bf16[512,64]{0,1:T(8,128)(2,1)S(1)} %get-tuple-element.11), channel_id=1, source_target_pairs={{0,1},{1,0},{2,3},{3,2},{4,5},{5,4},{6,7},{7,6},{8,9},{9,8},{10,11... | collective-permute-start | bytes 196616 | tf_op jit(solution)/shard_map/ppermute | solution.py:21
  180.4 4.4 %collective-permute-start = (bf16[512,64]{0,1:T(8,128)(2,1)S(1)}, bf16[512,64]{0,1:T(8,128)(2,1)S(1)}, u32[]{:S(2)}, u32[]{:S(2)}) collective-permute-start(bf16[512,64]{0,1:T(8,128)(2,1)S(1)} %fusion.39), channel_id=1, source_target_pairs={{0,1},{1,0},{2,3},{3,2},{4,5},{5,4},{6,7},{7,6},{8,9},{9,8},{10,11... | collective-permute-start | bytes 196616 | tf_op jit(solution)/shard_map/ppermute | solution.py:21
  212.3 0.7 copy-start.3
  212.3 0.7 copy-start.1
  212.3 13.1 %copy-start.4 = (s32[1,32]{1,0:T(1,128)S(1)}, s32[1,32]{1,0:T(1,128)}, u32[]{:S(2)}) copy-start(s32[1,32]{1,0:T(1,128)} %param.19) | copy-start | bytes 388
  212.3 113.3 %copy-start = (bf16[512,512]{1,0:T(8,128)(2,1)S(1)}, bf16[512,512]{1,0:T(8,128)(2,1)}, u32[]{:S(2)}) copy-start(bf16[512,512]{1,0:T(8,128)(2,1)} %param.10) | copy-start | bytes 1572868
  215.4 23.6 %all-to-all-start = ((bf16[8,6,2048]{2,1,0:T(8,128)(2,1)}), bf16[8,6,2048]{2,1,0:T(8,128)(2,1)S(1)}, u32[]{:S(2)}, u32[]{:S(2)}) async-start(bf16[8,6,2048]{2,1,0:T(8,128)(2,1)} %reshape.281), calls=%async_computation.1 | async-start | bytes 524288 | tf_op jit(solution)/shard_map/all_to_all | solution.py:134
  239.0 15.5 %collective-permute-start.2 = (bf16[8,6,2048]{2,1,0:T(8,128)(2,1)S(1)}, bf16[8,6,2048]{2,1,0:T(8,128)(2,1)S(1)}, u32[]{:S(2)}, u32[]{:S(2)}) collective-permute-start(bf16[8,6,2048]{2,1,0:T(8,128)(2,1)S(1)} %all-to-all-done), channel_id=1, source_target_pairs={{0,128},{128,0},{1,129},{129,1},{2,130},{130,2},{3,131},{131,3},{4... | collective-permute-start | bytes 589832 | tf_op jit(solution)/shard_map/ppermute | solution.py:27
  252.7 1.2 collective-permute-start.3
Sparse Core Ops, SparseCore 0:
  9.8 105.6 all-gather.6
  117.3 21.8 all-gather.12
  141.0 15.6 all-gather.10
  158.3 15.6 all-gather.8
  175.7 26.4 all-gather.14
  212.5 113.0 reduce-scatter.1
where the time goes:
time: 335 us; the launch traced here: 334 us
  waiting for transfers between devices  196 us (59%)
  blocking collectives  57.6 us (17%)
  matrix products  35.7 us (11%)
  between operations  15 us (4%)
  starting transfers between devices  13.5 us (4%)
  other arithmetic  11.8 us (4%)
  local copies, waits for them, and re-layouts  4.39 us (1%)
    reduce_scatter x1, waiting for transfers between devices, shards(): lax.psum_scatter(terms.astype(jnp.bfloat16), 'tp', scatter_dimension=1, t...  70.3 us
    all_gather x1, waiting for transfers between devices, shards(): lax.all_gather(tokens, 'tp', axis=1, tiled=True)  59.1 us
    all_gather x1, blocking collectives, shards(): lax.all_gather(norm_gain, 'tp', axis=0, tiled=True)  44 us
    dot_general x3, matrix products, shards(): jnp.dot(normed, piece, preferred_element_type=jnp.float32)  24 us
    all_gather x1, waiting for transfers between devices, shards(): lax.all_gather(wq, 'side', axis=0, tiled=True)  18.6 us
    all_to_all x1, blocking collectives, shards(): lax.all_to_all(id_buffer, 'grp', split_axis=0, concat_axis=0, tiled=True)  13.6 us
    all_to_all x1, waiting for transfers between devices, shards(): lax.all_to_all(buffer, 'grp', split_axis=0, concat_axis=0, tiled=True)  13.5 us
    all_gather x1, waiting for transfers between devices, shards(): lax.all_gather(wo, 'side', axis=1, tiled=True)  13.3 us
  transfers between devices with their start and end apart: 11, of which 9 were waited for; matrix products, arithmetic and copies ran while one was open for 12% of the time, Pallas kernels for 0%

commit v1 on v0

--- a/solution.py
+++ b/solution.py
@@ -1,14 +1,275 @@
 import jax
 import jax.numpy as jnp
 from jax import lax
+from jax.experimental import pallas as pl
+from jax.experimental.pallas import tpu as pltpu
 from jax.sharding import PartitionSpec as P
 
 KVH = 8
 HD = 128
 PAGE = 16
-
-
 EPS = 1e-05
+F32 = jnp.float32
+BF16 = jnp.bfloat16
+MESH = pl.DeviceIdType.MESH
+VMEM = pltpu.VMEM
+
+TOK = 512
+COLS = 512
+KCOLS = 64
+NH = 2
+RH = TOK // NH
+NU = 2 * NH
+NK = 2 * NU
+
+
+def place():
+    core = lax.axis_index("side")
+    tp = lax.axis_index("tp")
+    z = tp // 4
+    y = lax.rem(tp, 4)
+    m = jnp.where(core == 0, z, 3 - z)
+    return core, z, y, m
+
+
+def at_m(core, m, y):
+    z = jnp.where(core == 0, m, 3 - m)
+    return z * 4 + y
+
+
+def greet(core, z, y, extra=()):
+    barrier = pltpu.get_barrier_semaphore()
+    near = [
+        {"tp": lax.rem(z + 1, 4) * 4 + y},
+        {"tp": lax.rem(z + 3, 4) * 4 + y},
+        {"tp": z * 4 + lax.rem(y + 1, 4)},
+        {"tp": z * 4 + lax.rem(y + 3, 4)},
+        {"side": 1 - core},
+    ]
+    for one in near:
+        pl.semaphore_signal(barrier, inc=1, device_id=one, device_id_type=MESH)
+    count = len(near)
+    return barrier, count
+
+
+def gather_kernel(
+    tok_ref, gain_ref, wq_hbm, wk_ref, wv_ref, q_ref, kv_ref,
+    blocks, own, wq_v, wkv_v, acc_q, acc_kv, got_q, got_kv,
+    w_sem, d_send, d_recv, up_send, up_recv, dn_send, dn_recv,
+    yp_send, yp_recv, ym_send, ym_recv, fw_send, fw_recv, x_send, x_recv,
+):
+    core, z, y, m = place()
+    root = z // 2
+    weights = pltpu.make_async_copy(wq_hbm, wq_v, w_sem)
+    weights.start()
+    barrier, count = greet(core, z, y)
+    own_zz = lax.rem(z, 2)
+
+    for h in range(NH):
+        scaled = (
+            tok_ref[h * RH:(h + 1) * RH, :].astype(F32) * gain_ref[...].astype(F32)
+        ).astype(BF16)
+        own[h] = scaled
+
+    def to_root(h):
+        return pltpu.make_async_remote_copy(
+            src_ref=own.at[h], dst_ref=blocks.at[own_zz, y, core, h],
+            send_sem=d_send.at[h], recv_sem=d_recv.at[h],
+            device_id={"side": 1 - core}, device_id_type=MESH,
+        )
+
+    pl.semaphore_wait(barrier, count)
+
+    @pl.when(root != core)
+    def _():
+        for h in range(NH):
+            to_root(h).start()
+
+    @pl.when(root == core)
+    def _():
+        for h in range(NH):
+            blocks[own_zz, y, core, h] = own[h]
+
+    acc_q[...] = jnp.zeros_like(acc_q)
+    acc_kv[...] = jnp.zeros_like(acc_kv)
+    wkv_v[:, :, :, :KCOLS] = wk_ref[...]
+    wkv_v[:, :, :, KCOLS:] = wv_ref[...]
+
+    up = {"tp": at_m(core, lax.rem(m + 1, 4), y)}
+    down = {"tp": at_m(core, lax.rem(m + 3, 4), y)}
+    yp = {"tp": z * 4 + lax.rem(y + 1, 4)}
+    ym = {"tp": z * 4 + lax.rem(y + 3, 4)}
+    y1, y2, y3 = lax.rem(y + 1, 4), lax.rem(y + 2, 4), lax.rem(y + 3, 4)
+
+    def unit(k):
+        u = k // 2
+        b = 1 - lax.rem(k, 2)
+        zz = jnp.where(core == 0, b, 1 - b)
+        first = u == 0
+        mid = u <= NH
+        side = jnp.where(first, core, jnp.where(mid, 1 - core, core))
+        h = jnp.where(first, 0, jnp.where(mid, u - 1, u - NH))
+        return b, zz, side, h
+
+    def copy(ref, send, recv, to):
+        return pltpu.make_async_remote_copy(
+            src_ref=ref, dst_ref=ref, send_sem=send, recv_sem=recv,
+            device_id=to, device_id_type=MESH,
+        )
+
+    def line(k):
+        b, zz, side, h = unit(k)
+        ref = blocks.at[zz, y, side, h]
+        is_root = m == b
+
+        @pl.when(is_root & (side != core))
+        def _():
+            copy(ref, d_send.at[h], d_recv.at[h], {"side": 1 - core}).wait_recv()
+
+        @pl.when(m > b)
+        def _():
+            copy(ref, up_send.at[k], up_recv.at[k], up).wait_recv()
+
+        @pl.when(m < b)
+        def _():
+            copy(ref, dn_send.at[k], dn_recv.at[k], down).wait_recv()
+
+        @pl.when((m >= b) & (m < 3))
+        def _():
+            copy(ref, up_send.at[k], up_recv.at[k], up).start()
+
+        @pl.when((m == 1) & (b == 1))
+        def _():
+            copy(ref, dn_send.at[k], dn_recv.at[k], down).start()
+
+        copy(ref, yp_send.at[k], yp_recv.at[k], yp).start()
+        copy(ref, ym_send.at[k], ym_recv.at[k], ym).start()
+
+    def ring(k):
+        b, zz, side, h = unit(k)
+        low = blocks.at[zz, y3, side, h]
+        high = blocks.at[zz, y1, side, h]
+        copy(low, yp_send.at[k], yp_recv.at[k], yp).wait_recv()
+
+        @pl.when(lax.rem(h, 2) == 0)
+        def _():
+            copy(low, fw_send.at[k], fw_recv.at[k], yp).start()
+
+        copy(high, ym_send.at[k], ym_recv.at[k], ym).wait_recv()
+
+        @pl.when(lax.rem(h, 2) == 1)
+        def _():
+            copy(high, fw_send.at[k], fw_recv.at[k], ym).start()
+
+    def swap(which):
+        if which == 0:
+            return pltpu.make_async_remote_copy(
+                src_ref=acc_q.at[1 - core], dst_ref=got_q, send_sem=x_send.at[0],
+                recv_sem=x_recv.at[0], device_id={"side": 1 - core}, device_id_type=MESH)
+        return pltpu.make_async_remote_copy(
+            src_ref=acc_kv.at[1 - core], dst_ref=got_kv, send_sem=x_send.at[1],
+            recv_sem=x_recv.at[1], device_id={"side": 1 - core}, device_id_type=MESH)
+
+    def multiply(k):
+        b, zz, side, h = unit(k)
+        far = blocks.at[zz, y2, side, h]
+        copy(far, fw_send.at[k], fw_recv.at[k], yp).wait_recv()
+        rows = pl.ds(pl.multiple_of(h * RH, RH), RH)
+        total_q = acc_q[side, rows, :]
+        total_kv = acc_kv[side, rows, :]
+        for yy in range(4):
+            x = blocks[zz, yy, side, h]
+            total_q += jnp.dot(x, wq_v[zz, yy], preferred_element_type=F32)
+            total_kv += jnp.dot(x, wkv_v[zz, yy], preferred_element_type=F32)
+        acc_q[side, rows, :] = total_q
+        acc_kv[side, rows, :] = total_kv
+
+        @pl.when(k == 2 * NH + 1)
+        def _():
+            swap(0).start()
+            swap(1).start()
+
+    LAG = 2
+    weights.wait()
+
+    def step(k, carry):
+        @pl.when(k < NK)
+        def _():
+            line(k)
+
+        @pl.when((k >= LAG) & (k < NK + LAG))
+        def _():
+            ring(k - LAG)
+
+        @pl.when(k >= LAG + 1)
+        def _():
+            multiply(k - LAG - 1)
+        return carry
+
+    lax.fori_loop(0, NK + LAG + 1, step, 0)
+
+    swap(0).wait()
+    swap(1).wait()
+    q_ref[...] = acc_q[core] + got_q[...]
+    kv_ref[...] = acc_kv[core] + got_kv[...]
+
+    @pl.when(root != core)
+    def _():
+        for h in range(NH):
+            to_root(h).wait_send()
+
+    def drain(k, carry):
+        b, zz, side, h = unit(k)
+        ref = blocks.at[zz, y, side, h]
+
+        @pl.when((m >= b) & (m < 3))
+        def _():
+            copy(ref, up_send.at[k], up_recv.at[k], up).wait_send()
+
+        @pl.when((m == 1) & (b == 1))
+        def _():
+            copy(ref, dn_send.at[k], dn_recv.at[k], down).wait_send()
+
+        copy(ref, yp_send.at[k], yp_recv.at[k], yp).wait_send()
+        copy(ref, ym_send.at[k], ym_recv.at[k], ym).wait_send()
+        copy(ref, fw_send.at[k], fw_recv.at[k], yp).wait_send()
+        return carry
+
+    lax.fori_loop(0, NK, drain, 0)
+
+
+def gather_project(tokens, gain, wq, wk, wv):
+    sem = pltpu.SemaphoreType.DMA
+    vm = pl.BlockSpec(memory_space=VMEM)
+    return pl.pallas_call(
+        gather_kernel,
+        out_shape=(
+            jax.ShapeDtypeStruct((TOK, COLS), F32),
+            jax.ShapeDtypeStruct((TOK, 2 * KCOLS), F32),
+        ),
+        in_specs=[vm, vm, pl.BlockSpec(memory_space=pl.ANY), vm, vm],
+        out_specs=(vm, vm),
+        scratch_shapes=[
+            VMEM((2, 4, 2, NH, RH, COLS), BF16),
+            VMEM((NH, RH, COLS), BF16),
+            VMEM((2, 4, COLS, COLS), BF16),
+            VMEM((2, 4, COLS, 2 * KCOLS), BF16),
+            VMEM((2, TOK, COLS), F32),
+            VMEM((2, TOK, 2 * KCOLS), F32),
+            VMEM((TOK, COLS), F32),
+            VMEM((TOK, 2 * KCOLS), F32),
+            sem, sem((NH,)), sem((NH,)),
+        ] + [sem((NK,))] * 10 + [sem((2,)), sem((2,))],
+        compiler_params=pltpu.CompilerParams(
+            collective_id=0, has_side_effects=True, vmem_limit_bytes=48 * 2**20
+        ),
+        cost_estimate=pl.CostEstimate(
+            flops=2 * 1024 * 4096 * 640, bytes_accessed=8 * 2**20, transcendentals=0
+        ),
+    )(
+        tokens, gain.reshape(1, COLS), wq.reshape(2, 4, COLS, COLS),
+        wk.reshape(2, 4, COLS, KCOLS), wv.reshape(2, 4, COLS, KCOLS),
+    )
 
 
 def partner(block, axis, apart):
@@ -43,25 +304,17 @@
 
 
 def shards(tokens, norm_gain, wq, wk, wv, wo, span_offsets, shared_pages, page_owner, page_ids):
-    whole, gain = (
-        lax.all_gather(tokens, "tp", axis=1, tiled=True),
-        lax.all_gather(norm_gain, "tp", axis=0, tiled=True),
-    )
-    count = whole.shape[0]
-    xf = whole.astype(jnp.float32)
-    normed = (
-        xf * lax.rsqrt(jnp.mean(xf * xf, axis=-1, keepdims=True) + EPS) * gain.astype(jnp.float32)
-    ).astype(jnp.bfloat16)
+    count = tokens.shape[0]
+    xf = tokens.astype(F32)
+    squares = lax.psum(jnp.sum(xf * xf, axis=1, keepdims=True), "tp")
+    q_raw, kv_raw = gather_project(tokens, norm_gain, wq, wk, wv)
+    scale = lax.rsqrt(squares / 8192.0 + EPS)
     qcols = wq.shape[1]
     kcols = wk.shape[1]
-    pieces = (
-        lax.all_gather(wq, "side", axis=0, tiled=True),
-        lax.all_gather(wk, "side", axis=0, tiled=True),
-        lax.all_gather(wv, "side", axis=0, tiled=True),
-    )
-    q_raw, k_raw, v_raw = tuple(
-        (jnp.dot(normed, piece, preferred_element_type=jnp.float32) for piece in pieces)
-    )
+    q_raw = q_raw * scale
+    kv_raw = kv_raw * scale
+    k_raw = kv_raw[:, :kcols]
+    v_raw = kv_raw[:, kcols:]
     positions = span_offsets[0] + jnp.arange(count, dtype=jnp.int32)
     tp_index = lax.axis_index("tp")
     sharing = lax.axis_size("tp") // KVH

time: 335 us -> 293 us (0.87)
  waiting for transfers between devices: 196 us -> 87 us
  Pallas kernels: 0 us -> 91.9 us
  matrix products: 35.7 us -> 11.7 us
  other arithmetic: 11.8 us -> 8.16 us
  local copies, waits for them, and re-layouts: 4.39 us -> 7.9 us
    all_gather x4 -> x0, waiting for transfers between devices: 92.3 us -> none  [the longest x1 59.1 us: shards(): lax.all_gather(tokens, 'tp', axis=1, tiled=True)]
    pallas_call x0 -> x1, Pallas kernels: none -> 91.9 us  [gather_project(): pl.pallas_call(gather_kernel, out_shape=(jax.ShapeDtypeStruct((TOK, COLS)...]
    psum x0 -> x1, blocking collectives: none -> 44.9 us  [shards(): squares = lax.psum(jnp.sum(xf * xf, axis=1, keepdims=True), 'tp')]
    all_gather x1 -> x0, blocking collectives: 44 us -> none  [shards(): lax.all_gather(norm_gain, 'tp', axis=0, tiled=True)]
    dot_general x3 -> x0, matrix products: 24 us -> none  [shards(): jnp.dot(normed, piece, preferred_element_type=jnp.float32)]
    all_gather x1, waiting for transfers between devices: 13.3 us -> 0.02 us  [shards(): lax.all_gather(wo, 'side', axis=1, tiled=True)]
    reduce_sum x1, other arithmetic: 5.1 us -> 0.18 us  [shards(): squares = lax.psum(jnp.sum(xf * xf, axis=1, keepdims=True), 'tp')]
    reduce_scatter x1, waiting for transfers between devices: 70.3 us -> 74.8 us  [shards(): lax.psum_scatter(terms.astype(jnp.bfloat16), 'tp', scatter_dimension=1, t...]
  transfers between devices with their start and end apart: 11 -> 7, of which waited for: 9 -> 4; matrix products, arithmetic and copies ran while one was open for 12% -> 5% of each run, Pallas kernels for 0% -> 31%
where the time goes in v1:
time: 293 us; the launch traced here: 292 us
  Pallas kernels  91.9 us (31%)
  waiting for transfers between devices  87 us (30%)
  blocking collectives  57.8 us (20%)
  between operations  15 us (5%)
  starting transfers between devices  12.8 us (4%)
  matrix products  11.7 us (4%)
  other arithmetic  8.16 us (3%)
  local copies, waits for them, and re-layouts  7.9 us (3%)
    pallas_call x1, Pallas kernels, gather_project(): pl.pallas_call(gather_kernel, out_shape=(jax.ShapeDtypeStruct((TOK, COLS)...  91.9 us
    reduce_scatter x1, waiting for transfers between devices, shards(): lax.psum_scatter(terms.astype(jnp.bfloat16), 'tp', scatter_dimension=1, t...  74.8 us
    psum x1, blocking collectives, shards(): squares = lax.psum(jnp.sum(xf * xf, axis=1, keepdims=True), 'tp')  44.9 us
    all_to_all x1, blocking collectives, shards(): lax.all_to_all(id_buffer, 'grp', split_axis=0, concat_axis=0, tiled=True)  12.9 us
    all_to_all x1, starting transfers between devices, shards(): lax.all_to_all(buffer, 'grp', split_axis=0, concat_axis=0, tiled=True)  10.6 us
    dot_general x1, matrix products, shards(): jnp.dot(context, lax.all_gather(wo, 'side', axis=1, tiled=True), preferre...  10.1 us
    all_to_all x1, waiting for transfers between devices, shards(): lax.all_to_all(buffer, 'grp', split_axis=0, concat_axis=0, tiled=True)  9.32 us
  transfers between devices with their start and end apart: 7, of which 4 were waited for; matrix products, arithmetic and copies ran while one was open for 5% of the time, Pallas kernels for 31%

profile of v1, /device:TPU:2, one launch (start us, length us, event | category | flops | bytes accessed | tf_op | source)
XLA Modules:
  0.0 292.2 jit_solution(1795095581633020538)
XLA Ops:
  7.2 0.7 all-gather.2.cloned.1.call-update
  8.0 0.2 copy-done.2
  8.2 0.5 copy.40
  8.7 1.4 copy.41
  10.3 44.9 %psum.7 = f32[512,1]{0,1:T(1,128)S(1)} all-reduce(f32[512,1]{0,1:T(1,128)S(1)} %bitcast.59), channel_id=1, replica_groups=mesh['side'=2,'grp'=8,'tp'=16] {'tp'}, use_global_device_ids=true, to_apply=%region_1.0 | all-reduce | flops 512 | bytes 4096 | tf_op jit(solution)/shard_map/psum | solution.py:309
  55.2 1.2 copy-done.1
  56.4 91.9 %shard_map.121 = (f32[512,512]{1,0:T(8,128)S(1)}, f32[512,128]{1,0:T(8,128)S(1)}) custom-call(bf16[512,512]{1,0:T(8,128)(2,1)S(1)} %copy-done, bf16[1,512]{1,0:T(2,128)(2,1)S(1)} %reshape.281.gain_ref, bf16[2,4,512,512]{3,2,1,0:T(8,128)(2,1)} %bitcast.63, bf16[2,4,512,64]{3,2,1,0:T(8,128)(2,1)S(1)} %bitcast.49, bf16[2,4,512,64]{3,2,1,0:T(8,128)(2,1)S(1)} %bitcast.50), custom_call_target="tpu_custom_call" | custom-call | flops 5368709120 | bytes 8388608 | tf_op jit(solution)/shard_map/pallas_call | solution.py:244
  148.7 2.0 collective-permute-start.1
  151.5 0.4 reshape.285
  151.9 1.0 multiply_cosine_fusion
  152.9 0.6 fusion.33
  153.5 0.3 subtract_convert_fusion
  154.0 1.0 collective-permute-done.1
  155.1 0.2 maximum_select_fusion.1
  155.3 1.2 fusion.18
  156.5 0.8 fusion.9
  157.3 2.1 fusion.35
  159.4 0.5 fusion.6
  159.9 10.1 %convolution_convert_fusion = bf16[512,8192]{1,0:T(8,128)(2,1)} fusion(bf16[512,512]{0,1:T(8,128)(2,1)S(1)} %bitcast.53, bf16[512,8192]{1,0:T(8,128)(2,1)} %all-gather.2.cloned.1.call-done), kind=kOutput, calls=%fused_computation.1 | convolution fusion | flops 4299161600 | bytes 17301504 | tf_op jit(solution)/shard_map/dot_general | solution.py:352
  170.1 0.6 copy-done.6
  171.4 0.3 copy.46
  171.7 0.3 reshape.287
  172.0 0.3 convolution_convert_fusion.1
  172.3 0.8 reshape.288
  173.1 10.6 %all-to-all-start = ((bf16[8,6,2048]{2,1,0:T(8,128)(2,1)}), bf16[8,6,2048]{2,1,0:T(8,128)(2,1)S(1)}, u32[]{:S(2)}, u32[]{:S(2)}) async-start(bf16[8,6,2048]{2,1,0:T(8,128)(2,1)} %reshape.288), calls=%async_computation.1 | async-start | bytes 524288 | tf_op jit(solution)/shard_map/all_to_all | solution.py:387
  183.8 9.3 %all-to-all-done = bf16[8,6,2048]{2,1,0:T(8,128)(2,1)S(1)} async-done(((bf16[8,6,2048]{2,1,0:T(8,128)(2,1)}), bf16[8,6,2048]{2,1,0:T(8,128)(2,1)S(1)}, u32[]{:S(2)}, u32[]{:S(2)}) %all-to-all-start) | async-done | bytes 196640 | tf_op jit(solution)/shard_map/all_to_all | solution.py:387
  193.2 12.9 %all_to_all.14 = s32[8,1,6]{2,1,0:T(1,128)S(1)} all-to-all(s32[8,1,6]{2,1,0:T(1,128)S(1)} %bitcast.58), channel_id=1, replica_groups=mesh['side'=2,'grp'=8,'tp'=16] {'grp'}, dimensions={0} | all-to-all | bytes 384 | tf_op jit(solution)/shard_map/all_to_all | solution.py:388
  206.1 1.2 collective-permute-done.3
  207.2 0.6 reshape.290
  207.8 0.7 reshape.289
  208.6 74.8 %reduce-scatter.2.cloned.1.call-done = bf16[512,512]{1,0:T(8,128)(2,1)} async-done(((bf16[512,8192]{1,0:T(8,128)(2,1)}), bf16[512,512]{1,0:T(8,128)(2,1)}) %reduce-scatter.2.cloned.1.call-update) | async-done | bytes 524304 | tf_op jit(solution)/shard_map/reduce_scatter | solution.py:355
  283.4 2.0 fusion.8
  (47 shorter events, 1.9 us)
Async XLA Ops:
  7.2 0.8 copy-start.5
  7.2 1.0 copy-start.2
  7.2 1.5 copy-start.3
  7.2 2.9 copy-start
  7.2 152.7 %all-gather.2.cloned.1.call-start = ((), (), s32[]{:S(2)}) async-start(), calls=%async_computation.3 | async-start | bytes 12582912 | tf_op jit(solution)/shard_map/all_gather | solution.py:353
  7.9 275.4 %reduce-scatter.2.cloned.1.call-start = ((), (), s32[]{:S(2)}) async-start(), calls=%async_computation.4 | async-start | bytes 8912896 | tf_op jit(solution)/shard_map/reduce_scatter | solution.py:355
  55.2 1.2 copy-start.1
  148.6 5.3 %collective-permute-start = (bf16[512,64]{1,0:T(8,128)(2,1)S(1)}, bf16[512,64]{1,0:T(8,128)(2,1)S(1)}, u32[]{:S(2)}, u32[]{:S(2)}) collective-permute-start(bf16[512,64]{1,0:T(8,128)(2,1)S(1)} %get-tuple-element.13), channel_id=1, source_target_pairs={{0,1},{1,0},{2,3},{3,2},{4,5},{5,4},{6,7},{7,6},{8,9},{9,8},{10,11... | collective-permute-start | bytes 196616 | tf_op jit(solution)/shard_map/ppermute | solution.py:282
  148.7 6.4 %collective-permute-start.1 = (bf16[512,64]{1,0:T(8,128)(2,1)S(1)}, bf16[512,64]{1,0:T(8,128)(2,1)S(1)}, u32[]{:S(2)}, u32[]{:S(2)}) collective-permute-start(bf16[512,64]{1,0:T(8,128)(2,1)S(1)} %get-tuple-element.14), channel_id=1, source_target_pairs={{0,1},{1,0},{2,3},{3,2},{4,5},{5,4},{6,7},{7,6},{8,9},{9,8},{10,11... | collective-permute-start | bytes 196616 | tf_op jit(solution)/shard_map/ppermute | solution.py:282
  170.0 0.7 copy-start.6
  170.0 0.7 copy-start.4
  170.0 13.6 %copy-start.7 = (s32[1,32]{1,0:T(1,128)S(1)}, s32[1,32]{1,0:T(1,128)}, u32[]{:S(2)}) copy-start(s32[1,32]{1,0:T(1,128)} %param.19) | copy-start | bytes 388
  173.1 20.0 %all-to-all-start = ((bf16[8,6,2048]{2,1,0:T(8,128)(2,1)}), bf16[8,6,2048]{2,1,0:T(8,128)(2,1)S(1)}, u32[]{:S(2)}, u32[]{:S(2)}) async-start(bf16[8,6,2048]{2,1,0:T(8,128)(2,1)} %reshape.288), calls=%async_computation.1 | async-start | bytes 524288 | tf_op jit(solution)/shard_map/all_to_all | solution.py:387
  193.1 14.8 %collective-permute-start.2 = (bf16[8,6,2048]{2,1,0:T(8,128)(2,1)S(1)}, bf16[8,6,2048]{2,1,0:T(8,128)(2,1)S(1)}, u32[]{:S(2)}, u32[]{:S(2)}) collective-permute-start(bf16[8,6,2048]{2,1,0:T(8,128)(2,1)S(1)} %all-to-all-done), channel_id=1, source_target_pairs={{0,128},{128,0},{1,129},{129,1},{2,130},{130,2},{3,131},{131,3},{4... | collective-permute-start | bytes 589832 | tf_op jit(solution)/shard_map/ppermute | solution.py:288
  206.1 1.2 collective-permute-start.3
Sparse Core Ops, SparseCore 0:
  9.8 28.1 all-gather.1
  170.2 113.1 reduce-scatter.1

commit v2 on v1

--- a/solution.py
+++ b/solution.py
@@ -21,6 +21,9 @@
 RH = TOK // NH
 NU = 2 * NH
 NK = 2 * NU
+WO_Z = 1
+WO_X = 3
+WO_D = 8
 
 
 def place():
@@ -37,15 +40,8 @@
     return z * 4 + y
 
 
-def greet(core, z, y, extra=()):
+def greet(near):
     barrier = pltpu.get_barrier_semaphore()
-    near = [
-        {"tp": lax.rem(z + 1, 4) * 4 + y},
-        {"tp": lax.rem(z + 3, 4) * 4 + y},
-        {"tp": z * 4 + lax.rem(y + 1, 4)},
-        {"tp": z * 4 + lax.rem(y + 3, 4)},
-        {"side": 1 - core},
-    ]
     for one in near:
         pl.semaphore_signal(barrier, inc=1, device_id=one, device_id_type=MESH)
     count = len(near)
@@ -53,16 +49,26 @@
 
 
 def gather_kernel(
-    tok_ref, gain_ref, wq_hbm, wk_ref, wv_ref, q_ref, kv_ref,
-    blocks, own, wq_v, wkv_v, acc_q, acc_kv, got_q, got_kv,
+    tok_ref, gain_ref, wq_hbm, wk_ref, wv_ref, wo_hbm, q_ref, kv_ref, wo_all,
+    sq, blocks, own, wq_v, wkv_v, acc_q, acc_kv, got_q, got_kv,
     w_sem, d_send, d_recv, up_send, up_recv, dn_send, dn_recv,
     yp_send, yp_recv, ym_send, ym_recv, fw_send, fw_recv, x_send, x_recv,
+    sy_send, sy_recv, sz_send, sz_recv,
+    wz_send, wz_recv, wx_send, wx_recv, wd_send, wd_recv, wl_sem,
 ):
     core, z, y, m = place()
     root = z // 2
     weights = pltpu.make_async_copy(wq_hbm, wq_v, w_sem)
     weights.start()
-    barrier, count = greet(core, z, y)
+    grp = lax.axis_index("grp")
+    x = grp // 2
+    z_hi = lax.rem(grp, 2)
+    home = z // 2 == core
+    z_near = [{"tp": lax.rem(z + d, 4) * 4 + y} for d in (1, 2, 3)]
+    y_near = [{"tp": z * 4 + lax.rem(y + d, 4)} for d in (1, 2, 3)]
+    x_near = [{"grp": lax.rem(x + d, 4) * 2 + z_hi} for d in (1, 2, 3)]
+    sibling = {"side": 1 - core}
+    barrier, count = greet(z_near + y_near + x_near + [sibling])
     own_zz = lax.rem(z, 2)
 
     for h in range(NH):
@@ -70,6 +76,11 @@
             tok_ref[h * RH:(h + 1) * RH, :].astype(F32) * gain_ref[...].astype(F32)
         ).astype(BF16)
         own[h] = scaled
+    xf = tok_ref[...].astype(F32)
+    sq[0] = lax.dot_general(
+        jnp.ones((8, COLS), F32), xf * xf, (((1,), (1,)), ((), ())),
+        precision=lax.Precision.HIGHEST, preferred_element_type=F32,
+    )
 
     def to_root(h):
         return pltpu.make_async_remote_copy(
@@ -90,6 +101,75 @@
         for h in range(NH):
             blocks[own_zz, y, core, h] = own[h]
 
+    def sum_y(d):
+        return pltpu.make_async_remote_copy(
+            src_ref=sq.at[0], dst_ref=sq.at[d], send_sem=sy_send.at[d - 1],
+            recv_sem=sy_recv.at[d - 1], device_id=y_near[d - 1], device_id_type=MESH)
+
+    def sum_z(d):
+        return pltpu.make_async_remote_copy(
+            src_ref=sq.at[4], dst_ref=sq.at[4 + d], send_sem=sz_send.at[d - 1],
+            recv_sem=sz_recv.at[d - 1], device_id=z_near[d - 1], device_id_type=MESH)
+
+    def wo_line(zz):
+        z_to = 2 * core + zz
+        return pltpu.make_async_remote_copy(
+            src_ref=wo_hbm.at[x, :, zz * 2048:(zz + 1) * 2048],
+            dst_ref=wo_all.at[z, x], send_sem=wz_send.at[zz], recv_sem=wz_recv.at[z],
+            device_id={"tp": z_to * 4 + y}, device_id_type=MESH)
+
+    def wo_row(d, e):
+        ref = wo_all.at[lax.rem(z + d, 4), x]
+        return pltpu.make_async_remote_copy(
+            src_ref=ref, dst_ref=ref, send_sem=wx_send.at[d - 1, e - 1],
+            recv_sem=wx_recv.at[d - 1, e - 1], device_id=x_near[e - 1], device_id_type=MESH)
+
+    own_cols = pl.ds(pl.multiple_of(own_zz * 2048, 2048), 2048)
+
+    def wo_local():
+        return pltpu.make_async_copy(wo_hbm.at[:, :, own_cols], wo_all.at[z], wl_sem)
+
+    def wo_cross(d):
+        here = wo_all.at[lax.rem(z + d, 4)]
+        return pltpu.make_async_remote_copy(
+            src_ref=wo_hbm.at[:, :, own_cols] if d == 0 else here, dst_ref=here,
+            send_sem=wd_send.at[d], recv_sem=wd_recv.at[d],
+            device_id=sibling, device_id_type=MESH)
+
+    def redistribute(k):
+        @pl.when(k == WO_Z)
+        def _():
+            for zz in range(2):
+                @pl.when(2 * core + zz != z)
+                def _():
+                    wo_line(zz).start()
+
+            @pl.when(home)
+            def _():
+                wo_local().start()
+                wo_cross(0).start()
+
+        for d in (1, 2, 3):
+            z_from = lax.rem(z + d, 4)
+
+            @pl.when(home & (k == WO_X + jnp.abs(z_from - z) - 1))
+            def _():
+                ref = wo_all.at[z_from, x]
+                pltpu.make_async_remote_copy(
+                    src_ref=ref, dst_ref=ref, send_sem=wz_send.at[0],
+                    recv_sem=wz_recv.at[z_from], device_id=z_near[d - 1],
+                    device_id_type=MESH).wait_recv()
+                for e in (1, 2, 3):
+                    wo_row(d, e).start()
+
+            @pl.when(home & (k == WO_D + jnp.abs(z_from - z) - 1))
+            def _():
+                for e in (1, 2, 3):
+                    wo_row(d, e).wait_recv()
+                wo_cross(d).start()
+
+    for d in (1, 2, 3):
+        sum_y(d).start()
     acc_q[...] = jnp.zeros_like(acc_q)
     acc_kv[...] = jnp.zeros_like(acc_kv)
     wkv_v[:, :, :, :KCOLS] = wk_ref[...]
@@ -204,14 +284,50 @@
         @pl.when(k >= LAG + 1)
         def _():
             multiply(k - LAG - 1)
+
+        redistribute(k)
+
+        @pl.when(k == 3)
+        def _():
+            for d in (1, 2, 3):
+                sum_y(d).wait_recv()
+            sq[4] = sq[0] + sq[1] + sq[2] + sq[3]
+            for d in (1, 2, 3):
+                sum_z(d).start()
         return carry
 
     lax.fori_loop(0, NK + LAG + 1, step, 0)
 
     swap(0).wait()
     swap(1).wait()
-    q_ref[...] = acc_q[core] + got_q[...]
-    kv_ref[...] = acc_kv[core] + got_kv[...]
+    for d in (1, 2, 3):
+        sum_z(d).wait_recv()
+    total = (sq[4] + sq[5] + sq[6] + sq[7]).T[:, :1]
+    scale = lax.rsqrt(total * (1.0 / 8192.0) + EPS)
+    q_ref[...] = (acc_q[core] + got_q[...]) * scale
+    kv_ref[...] = (acc_kv[core] + got_kv[...]) * scale
+
+    for d in (1, 2, 3):
+        sum_y(d).wait_send()
+        sum_z(d).wait_send()
+    for zz in range(2):
+        @pl.when(2 * core + zz != z)
+        def _():
+            wo_line(zz).wait_send()
+
+    @pl.when(home)
+    def _():
+        wo_local().wait()
+        for d in range(4):
+            wo_cross(d).wait_send()
+        for d in (1, 2, 3):
+            for e in (1, 2, 3):
+                wo_row(d, e).wait_send()
+
+    @pl.when(jnp.logical_not(home))
+    def _():
+        for d in range(4):
+            wo_cross(d).wait_recv()
 
     @pl.when(root != core)
     def _():
@@ -238,7 +354,7 @@
     lax.fori_loop(0, NK, drain, 0)
 
 
-def gather_project(tokens, gain, wq, wk, wv):
+def gather_project(tokens, gain, wq, wk, wv, wo):
     sem = pltpu.SemaphoreType.DMA
     vm = pl.BlockSpec(memory_space=VMEM)
     return pl.pallas_call(
@@ -246,10 +362,13 @@
         out_shape=(
             jax.ShapeDtypeStruct((TOK, COLS), F32),
             jax.ShapeDtypeStruct((TOK, 2 * KCOLS), F32),
+            jax.ShapeDtypeStruct((4, 4, 128, 2048), BF16),
         ),
-        in_specs=[vm, vm, pl.BlockSpec(memory_space=pl.ANY), vm, vm],
-        out_specs=(vm, vm),
+        in_specs=[vm, vm, pl.BlockSpec(memory_space=pl.ANY), vm, vm,
+                  pl.BlockSpec(memory_space=pl.ANY)],
+        out_specs=(vm, vm, pl.BlockSpec(memory_space=pl.ANY)),
         scratch_shapes=[
+            VMEM((8, 8, TOK), F32),
             VMEM((2, 4, 2, NH, RH, COLS), BF16),
             VMEM((NH, RH, COLS), BF16),
             VMEM((2, 4, COLS, COLS), BF16),
@@ -259,7 +378,10 @@
             VMEM((TOK, COLS), F32),
             VMEM((TOK, 2 * KCOLS), F32),
             sem, sem((NH,)), sem((NH,)),
-        ] + [sem((NK,))] * 10 + [sem((2,)), sem((2,))],
+        ] + [sem((NK,))] * 10 + [
+            sem((2,)), sem((2,)), sem((3,)), sem((3,)), sem((3,)), sem((3,)),
+            sem((2,)), sem((4,)), sem((3, 3)), sem((3, 3)), sem((4,)), sem((4,)), sem,
+        ],
         compiler_params=pltpu.CompilerParams(
             collective_id=0, has_side_effects=True, vmem_limit_bytes=48 * 2**20
         ),
@@ -269,23 +391,214 @@
     )(
         tokens, gain.reshape(1, COLS), wq.reshape(2, 4, COLS, COLS),
         wk.reshape(2, 4, COLS, KCOLS), wv.reshape(2, 4, COLS, KCOLS),
-    )
-
-
-def partner(block, axis, apart):
-    count = lax.axis_size(axis)
-    route = []
-    for low in range(count):
-        high = low | 1 << apart
-        if high != low and high < count:
-            route += [(low, high), (high, low)]
-    return lax.ppermute(block, axis, route)
-
-
-def from_behind(value, axis, steps):
-    count = lax.axis_size(axis)
-    pairs = [(source, (source + steps) % count) for source in range(count)]
-    return lax.ppermute(value, axis, pairs)
+        wo.reshape(4, 128, 4096),
+    )
+
+
+NT = 4
+RT = TOK // NT
+HT = RT // 2
+
+
+def output_kernel(
+    ctx_ref, tok_ref, wo_hbm, pages_ref, ids_ref, mixed_ref, pool_ref, pool_ids_ref,
+    ctx, wo, opp_out, opp_in, near_out, near_in, near_part, own_part,
+    w_sem, up_send, up_recv, dn_send, dn_recv, a_send, a_recv, b_send, b_recv,
+    p_send, p_recv, i_send, i_recv,
+):
+    core, z, y, m = place()
+    grp = lax.axis_index("grp")
+
+    def weights(zs, yy):
+        return pltpu.make_async_copy(
+            wo_hbm.at[zs, :, yy * COLS:(yy + 1) * COLS], wo.at[zs, yy], w_sem.at[zs, yy])
+
+    for zs in range(4):
+        for yy in range(4):
+            weights(zs, yy).start()
+    owners = [{"side": 1 - core, "grp": jnp.int32(o)} for o in range(8)]
+    up = {"tp": lax.rem(z + 1, 4) * 4 + y}
+    down = {"tp": lax.rem(z + 3, 4) * 4 + y}
+    yp = {"tp": z * 4 + lax.rem(y + 1, 4)}
+    ym = {"tp": z * 4 + lax.rem(y + 3, 4)}
+    barrier, count = greet([up, down, yp, ym] + owners)
+    ctx[z] = ctx_ref[...]
+    pl.semaphore_wait(barrier, count)
+
+    def copy(src, dst, send, recv, to):
+        return pltpu.make_async_remote_copy(
+            src_ref=src, dst_ref=dst, send_sem=send, recv_sem=recv,
+            device_id=to, device_id_type=MESH)
+
+    def climb(zs, t):
+        ref = ctx.at[zs, t]
+        return copy(ref, ref, up_send.at[zs, t], up_recv.at[zs, t], up)
+
+    def descend(zs, t):
+        ref = ctx.at[zs, t]
+        return copy(ref, ref, dn_send.at[zs, t], dn_recv.at[zs, t], down)
+
+    def opposite(t, way):
+        return copy(opp_out.at[t, way], opp_in.at[t, way], a_send.at[t, way],
+                    a_recv.at[t, way], (yp, ym)[way])
+
+    def neighbour(t, way):
+        return copy(near_out.at[t, way], near_in.at[t, way], b_send.at[t, way],
+                    b_recv.at[t, way], (yp, ym)[way])
+
+    def page(o):
+        return copy(pages_ref.at[o], pool_ref.at[grp], p_send.at[o], p_recv.at[grp], owners[o])
+
+    def page_id(o):
+        return copy(ids_ref.at[o], pool_ids_ref.at[grp], i_send.at[o], i_recv.at[grp], owners[o])
+
+    def launch(t):
+        @pl.when(z < 3)
+        def _():
+            climb(z, t).start()
+
+        @pl.when(z > 0)
+        def _():
+            descend(z, t).start()
+
+    def fetch(t):
+        @pl.when(t < NT - 1)
+        def _():
+            launch(t + 1)
+
+        for d in (1, 2, 3):
+            @pl.when(z - d >= 0)
+            def _():
+                climb(z - d, t).wait_recv()
+
+                @pl.when(z < 3)
+                def _():
+                    climb(z - d, t).start()
+
+            @pl.when(z + d <= 3)
+            def _():
+                descend(z + d, t).wait_recv()
+
+                @pl.when(z > 0)
+                def _():
+                    descend(z + d, t).start()
+
+    def product(t, r):
+        yy = lax.rem(y + r, 4)
+        total = jnp.dot(ctx[0, t], wo[0, yy], preferred_element_type=F32)
+        for zs in (1, 2, 3):
+            total += jnp.dot(ctx[zs, t], wo[zs, yy], preferred_element_type=F32)
+        return total
+
+    def compute(t):
+        far = product(t, 2).astype(BF16)
+        for way in (0, 1):
+            opp_out[t, way] = far[way * HT:(way + 1) * HT]
+            opposite(t, way).start()
+        near_part[t, 0] = product(t, 1)
+        near_part[t, 1] = product(t, 3)
+        own_part[t] = product(t, 0)
+
+    def pass_on(t):
+        for way in (0, 1):
+            opposite(t, way).wait_recv()
+            with_sum = slice(way * HT, (way + 1) * HT)
+            without = slice((1 - way) * HT, (2 - way) * HT)
+            near_out[t, way, with_sum, :] = (
+                near_part[t, way, with_sum, :] + opp_in[t, way].astype(F32)
+            ).astype(BF16)
+            near_out[t, way, without, :] = near_part[t, way, without, :].astype(BF16)
+            neighbour(t, way).start()
+
+    def finish(t):
+        neighbour(t, 0).wait_recv()
+        neighbour(t, 1).wait_recv()
+        total = own_part[t] + near_in[t, 0].astype(F32) + near_in[t, 1].astype(F32)
+        mixed_ref[t] = (tok_ref[t].astype(F32) + total).astype(BF16)
+
+    launch(0)
+    for o in range(8):
+        page(o).start()
+        page_id(o).start()
+    for zs in range(4):
+        for yy in range(4):
+            weights(zs, yy).wait()
+
+    def step(t, carry):
+        @pl.when(t < NT)
+        def _():
+            fetch(t)
+            compute(t)
+
+        @pl.when((t >= 1) & (t <= NT))
+        def _():
+            pass_on(t - 1)
+
+        @pl.when(t >= 2)
+        def _():
+            finish(t - 2)
+        return carry
+
+    lax.fori_loop(0, NT + 2, step, 0)
+
+    def drain(t, carry):
+        for zs in range(4):
+            @pl.when((z < 3) & (zs <= z))
+            def _():
+                climb(zs, t).wait_send()
+
+            @pl.when((z > 0) & (zs >= z))
+            def _():
+                descend(zs, t).wait_send()
+
+        for way in (0, 1):
+            opposite(t, way).wait_send()
+            neighbour(t, way).wait_send()
+        return carry
+
+    lax.fori_loop(0, NT, drain, 0)
+    for o in range(8):
+        page(o).wait_send()
+        page_id(o).wait_send()
+        copy(pages_ref.at[o], pool_ref.at[o], p_send.at[o], p_recv.at[o], owners[o]).wait_recv()
+        copy(ids_ref.at[o], pool_ids_ref.at[o], i_send.at[o], i_recv.at[o], owners[o]).wait_recv()
+
+
+def output_project(context, tokens, wo_all, pages, ids):
+    sem = pltpu.SemaphoreType.DMA
+    vm = pl.BlockSpec(memory_space=VMEM)
+    return pl.pallas_call(
+        output_kernel,
+        out_shape=(
+            jax.ShapeDtypeStruct((NT, RT, COLS), BF16),
+            jax.ShapeDtypeStruct(pages.shape, BF16),
+            jax.ShapeDtypeStruct(ids.shape, jnp.int32),
+        ),
+        in_specs=[vm, vm, pl.BlockSpec(memory_space=pl.ANY), vm, vm],
+        out_specs=(vm, vm, vm),
+        scratch_shapes=[
+            VMEM((4, NT, RT, COLS), BF16),
+            VMEM((4, 4, COLS, COLS), BF16),
+            VMEM((NT, 2, HT, COLS), BF16),
+            VMEM((NT, 2, HT, COLS), BF16),
+            VMEM((NT, 2, RT, COLS), BF16),
+            VMEM((NT, 2, RT, COLS), BF16),
+            VMEM((NT, 2, RT, COLS), F32),
+            VMEM((NT, RT, COLS), F32),
+            sem((4, 4)), sem((4, NT)), sem((4, NT)), sem((4, NT)), sem((4, NT)),
+            sem((NT, 2)), sem((NT, 2)), sem((NT, 2)), sem((NT, 2)),
+            sem((8,)), sem((8,)), sem((8,)), sem((8,)),
+        ],
+        compiler_params=pltpu.CompilerParams(
+            collective_id=1, has_side_effects=True, vmem_limit_bytes=48 * 2**20
+        ),
+        cost_estimate=pl.CostEstimate(
+            flops=2 * 512 * 2048 * 2048, bytes_accessed=10 * 2**20, transcendentals=0
+        ),
+    )(
+        context.reshape(NT, RT, COLS), tokens.reshape(NT, RT, COLS),
+        wo_all.reshape(4, COLS, 2048), pages, ids,
+    )
 
 
 def rotary(values, positions):
@@ -304,93 +617,60 @@
 
 
 def shards(tokens, norm_gain, wq, wk, wv, wo, span_offsets, shared_pages, page_owner, page_ids):
-    count = tokens.shape[0]
-    xf = tokens.astype(F32)
-    squares = lax.psum(jnp.sum(xf * xf, axis=1, keepdims=True), "tp")
-    q_raw, kv_raw = gather_project(tokens, norm_gain, wq, wk, wv)
-    scale = lax.rsqrt(squares / 8192.0 + EPS)
-    qcols = wq.shape[1]
-    kcols = wk.shape[1]
-    q_raw = q_raw * scale
-    kv_raw = kv_raw * scale
-    k_raw = kv_raw[:, :kcols]
-    v_raw = kv_raw[:, kcols:]
-    positions = span_offsets[0] + jnp.arange(count, dtype=jnp.int32)
-    tp_index = lax.axis_index("tp")
-    sharing = lax.axis_size("tp") // KVH
-    k_block = k_raw
-    v_block = v_raw
-    other_k = partner(k_block.astype(jnp.bfloat16), "tp", 0).astype(k_block.dtype)
-    other_v = partner(v_block.astype(jnp.bfloat16), "tp", 0).astype(v_block.dtype)
-    upper_half = tp_index // (1 << 0) % 2 == 1
-    k_block = jnp.where(
-        upper_half,
-        jnp.concatenate([other_k, k_block], axis=1),
-        jnp.concatenate([k_block, other_k], axis=1),
-    )
-    v_block = jnp.where(
-        upper_half,
-        jnp.concatenate([other_v, v_block], axis=1),
-        jnp.concatenate([v_block, other_v], axis=1),
-    )
-    query = rotary(q_raw.reshape(count, qcols // HD, HD), positions).astype(jnp.bfloat16)
-    keys = rotary(k_block.reshape(count, 1, HD), positions).astype(jnp.bfloat16).reshape(count, HD)
-    values = v_block.astype(jnp.bfloat16)
-    scores = jnp.einsum("qhd,kd->hqk", query, keys, preferred_element_type=jnp.float32) / jnp.sqrt(
-        jnp.float32(HD)
-    )
-    causal = jnp.arange(count)[:, None] >= jnp.arange(count)[None, :]
+    q_raw, kv_raw, wo_all = gather_project(tokens, norm_gain, wq, wk, wv, wo)
+    upper = lax.rem(lax.axis_index("tp"), 2) == 1
+    other = lax.ppermute(
+        kv_raw.astype(BF16), "tp", [(i, i ^ 1) for i in range(16)]
+    ).astype(F32)
+    low = jnp.where(upper, other, kv_raw)
+    high = jnp.where(upper, kv_raw, other)
+    k_raw = jnp.concatenate([low[:, :KCOLS], high[:, :KCOLS]], axis=1)
+    values = jnp.concatenate([low[:, KCOLS:], high[:, KCOLS:]], axis=1).astype(BF16)
+    positions = span_offsets[0] + jnp.arange(TOK, dtype=jnp.int32)
+    query = rotary(q_raw.reshape(TOK, COLS // HD, HD), positions).astype(BF16)
+    keys = rotary(k_raw.reshape(TOK, 1, HD), positions).astype(BF16).reshape(TOK, HD)
+
+    live = 1 - shared_pages[0]
+    owner = page_owner[0, :, 0]
+    onehot = (owner[:, None] == jnp.arange(8, dtype=jnp.int32)[None, :]).astype(
+        jnp.int32
+    ) * live[:, None]
+    rank = jnp.sum(jnp.cumsum(onehot, axis=0) * onehot, axis=1) - 1
+    slot = jnp.where(live == 1, owner * 6 + rank, -1)
+    select = slot[None, :] == jnp.arange(48, dtype=jnp.int32)[:, None]
+    ids = jnp.sum(select.astype(jnp.int32) * (page_ids[0] + 1)[None, :], axis=1) - 1
+    ids = jnp.pad(ids.reshape(8, 1, 6), ((0, 0), (0, 0), (0, 122)))
+    ids = jnp.broadcast_to(ids, (8, 8, 128))
+    row = (slot[:, None] * PAGE + jnp.arange(PAGE, dtype=jnp.int32)[None, :]).reshape(TOK)
+    picks = (row[None, :] == jnp.arange(768, dtype=jnp.int32)[:, None]).astype(BF16)
+    kv_own = jnp.concatenate(
+        [
+            jnp.where(upper, keys[:, KCOLS:], keys[:, :KCOLS]),
+            jnp.where(upper, values[:, KCOLS:], values[:, :KCOLS]),
+        ],
+        axis=1,
+    )
+    pages = jnp.dot(picks, kv_own, preferred_element_type=F32).astype(BF16).reshape(8, 96, 128)
+
+    scores = jnp.einsum("qhd,kd->hqk", query, keys, preferred_element_type=F32) / jnp.sqrt(
+        F32(HD)
+    )
+    causal = jnp.arange(TOK)[:, None] >= jnp.arange(TOK)[None, :]
     scores = jnp.where(causal[None], scores, -1e30)
     top = jnp.max(scores, axis=-1, keepdims=True)
     weights = jnp.exp(scores - top)
-    probs = (weights / jnp.sum(weights, axis=-1, keepdims=True)).astype(jnp.bfloat16)
+    probs = (weights / jnp.sum(weights, axis=-1, keepdims=True)).astype(BF16)
     context = (
-        jnp.einsum("hqk,kd->qhd", probs, values, preferred_element_type=jnp.float32)
-        .astype(jnp.bfloat16)
-        .reshape(count, qcols)
-    )
-    terms = jnp.dot(
-        context, lax.all_gather(wo, "side", axis=1, tiled=True), preferred_element_type=jnp.float32
-    )
-    attended = lax.psum_scatter(
-        terms.astype(jnp.bfloat16), "tp", scatter_dimension=1, tiled=True
-    ).astype(jnp.float32)
-    mixed = (tokens.astype(jnp.float32) + attended).astype(jnp.bfloat16)
-    pages_dev = count // PAGE
-    groups = lax.axis_size("grp")
-    cap = max(2, 3 * pages_dev // (2 * groups))
-    within_head = tp_index % sharing * kcols
-    k_own = lax.dynamic_slice_in_dim(keys, within_head, kcols, 1)
-    v_own = lax.dynamic_slice_in_dim(values, within_head, kcols, 1)
-    rows = jnp.stack(
-        [k_own.reshape(pages_dev, PAGE, kcols), v_own.reshape(pages_dev, PAGE, kcols)], axis=2
-    ).reshape(pages_dev, PAGE * 2 * kcols)
-    live = 1 - shared_pages[0]
-    owner = page_owner[0, :, 0]
-    onehot = (owner[:, None] == jnp.arange(groups, dtype=jnp.int32)[None, :]).astype(
-        jnp.int32
-    ) * live[:, None]
-    rank = jnp.sum(jnp.cumsum(onehot, axis=0) * onehot, axis=1) - 1
-    slots_count = groups * cap
-    select = (
-        (owner * cap + rank)[None, :] == jnp.arange(slots_count, dtype=jnp.int32)[:, None]
-    ) & (live[None, :] == 1)
-    buffer = jnp.dot(select.astype(jnp.bfloat16), rows, preferred_element_type=jnp.float32).astype(
-        jnp.bfloat16
-    )
-    id_buffer = jnp.sum(select.astype(jnp.int32) * (page_ids[0] + 1)[None, :], axis=1) - 1
-    buffer, id_buffer = (
-        buffer.reshape(slots_count // cap, cap, rows.shape[1]),
-        id_buffer.reshape(slots_count // cap, cap),
-    )
-    moved = (
-        lax.all_to_all(buffer, "grp", split_axis=0, concat_axis=0, tiled=True),
-        lax.all_to_all(id_buffer, "grp", split_axis=0, concat_axis=0, tiled=True),
-    )
-    got_pages, got_ids = from_behind((moved[0], moved[1]), "side", 1)
-    kv_pool = got_pages.reshape(groups * cap, rows.shape[1])
-    pool_ids = got_ids.reshape(groups * cap)
-    return (mixed, kv_pool, pool_ids)
+        jnp.einsum("hqk,kd->qhd", probs, values, preferred_element_type=F32)
+        .astype(BF16)
+        .reshape(TOK, COLS)
+    )
+    mixed, pool, pool_ids = output_project(context, tokens, wo_all, pages, ids)
+    return (
+        mixed.reshape(TOK, COLS),
+        pool.reshape(48, 2048),
+        pool_ids[:, 0, :6].reshape(48),
+    )
 
 
 def solution(mesh):

time: 293 us -> 207 us (0.71)
  Pallas kernels: 91.9 us -> 181 us
  waiting for transfers between devices: 87 us -> 0.01 us
  blocking collectives: 57.8 us -> 0 us
  between operations: 15 us -> 1.5 us
  starting transfers between devices: 12.8 us -> 2.33 us
  matrix products: 11.7 us -> 1.81 us
    reduce_scatter x1 -> x0, waiting for transfers between devices: 74.8 us -> none  [shards(): lax.psum_scatter(terms.astype(jnp.bfloat16), 'tp', scatter_dimension=1, t...]
    pallas_call x0 -> x1, Pallas kernels: none -> 58.8 us  [output_project(): pl.pallas_call(output_kernel, out_shape=(jax.ShapeDtypeStruct((NT, RT, CO...]
    psum x1 -> x0, blocking collectives: 44.9 us -> none  [shards(): squares = lax.psum(jnp.sum(xf * xf, axis=1, keepdims=True), 'tp')]
    pallas_call x1, Pallas kernels: 91.9 us -> 122 us  [gather_project(): pl.pallas_call(gather_kernel, out_shape=(jax.ShapeDtypeStruct((TOK, COLS)...]
    all_to_all x1 -> x0, blocking collectives: 12.9 us -> none  [shards(): lax.all_to_all(id_buffer, 'grp', split_axis=0, concat_axis=0, tiled=True)]
    all_to_all x1 -> x0, starting transfers between devices: 10.6 us -> none  [shards(): lax.all_to_all(buffer, 'grp', split_axis=0, concat_axis=0, tiled=True)]
    dot_general x4 -> x3, matrix products: 11.7 us -> 1.81 us  [the longest x1 0.79 us: shards(): jnp.einsum('qhd,kd->hqk', query, keys, preferred_element_type=F32)]
    all_to_all x1 -> x0, waiting for transfers between devices: 9.32 us -> none  [shards(): lax.all_to_all(buffer, 'grp', split_axis=0, concat_axis=0, tiled=True)]
  transfers between devices with their start and end apart: 7 -> 1, of which waited for: 4 -> 0; matrix products, arithmetic and copies ran while one was open for 5% -> 3% of each run, Pallas kernels for 31% -> 0%
where the time goes in v2:
time: 207 us; the launch traced here: 206 us
  Pallas kernels  181 us (87%)
  local copies, waits for them, and re-layouts  9.59 us (5%)
  other arithmetic  9.37 us (5%)
  starting transfers between devices  2.33 us (1%)
    pallas_call x1, Pallas kernels, gather_project(): pl.pallas_call(gather_kernel, out_shape=(jax.ShapeDtypeStruct((TOK, COLS)...  122 us
    pallas_call x1, Pallas kernels, output_project(): pl.pallas_call(output_kernel, out_shape=(jax.ShapeDtypeStruct((NT, RT, CO...  58.8 us
    unnamed x17, local copies, waits for them, and re-layouts  5.36 us
  transfers between devices with their start and end apart: 1, of which 0 were waited for; matrix products, arithmetic and copies ran while one was open for 3% of the time, Pallas kernels for 0%

profile of v2, /device:TPU:2, one launch (start us, length us, event | category | flops | bytes accessed | tf_op | source)
XLA Modules:
  0.0 205.8 jit_solution(17664988885345481884)
XLA Ops:
  0.6 1.5 copy.27
  2.2 1.5 copy.28
  3.7 0.7 reshape.248.gain_ref
  4.4 1.0 copy-done
  5.4 122.5 %shard_map.121 = (f32[512,512]{1,0:T(8,128)S(1)}, f32[512,128]{1,0:T(8,128)S(1)}, bf16[4,4,128,2048]{3,2,1,0:T(8,128)(2,1)}) custom-call(bf16[512,512]{1,0:T(8,128)(2,1)S(1)} %copy-done, bf16[1,512]{1,0:T(2,128)(2,1)S(1)} %reshape.248.gain_ref, bf16[2,4,512,512]{3,2,1,0:T(8,128)(2,1)} %bitcast.68, bf16[2,4,512,64]{3,2,1,0:T(8,128)(2,1)S(1)} %bitcast.59, ...), custom_call_target="tpu_custom_call" | custom-call | flops 5368709120 | bytes 8388608 | tf_op jit(solution)/shard_map/pallas_call | solution.py:360
  127.9 0.7 convert_element_type.35
  128.5 2.3 %collective-permute-start = (bf16[512,128]{1,0:T(8,128)(2,1)}, bf16[512,128]{1,0:T(8,128)(2,1)S(1)}, u32[]{:S(2)}, u32[]{:S(2)}) collective-permute-start(bf16[512,128]{1,0:T(8,128)(2,1)} %convert_element_type.35), channel_id=1, source_target_pairs={{0,1},{1,0},{2,3},{3,2},{4,5},{5,4},{6,7},{7,6},{8,9},{9,8},{10,11... | collective-permute-start | bytes 393224 | tf_op jit(solution)/shard_map/ppermute | solution.py:622
  130.9 0.5 multiply_exponential_fusion
  132.0 0.6 add_convert_fusion.1
  132.8 0.2 multiply_reduce_fusion
  133.1 0.4 copy-done.4
  133.5 0.4 reshape.254
  133.8 0.6 fusion.42
  134.5 0.7 fusion.34
  135.2 0.1 select_reduce_fusion
  135.3 0.7 sub.48
  136.0 1.7 multiply_cosine_fusion
  137.7 0.3 subtract_convert_fusion
  138.0 0.1 iota_compare_fusion.4
  138.2 0.1 broadcast_select_fusion
  138.3 0.1 maximum_bitcast_fusion
  138.5 1.9 broadcast_select_fusion.1
  140.4 0.8 fusion.11
  141.2 2.1 %fusion.43 = (f32[4,512]{1,0:T(4,128)S(1)}, f32[4,512,512]{1,2,0:T(8,128)S(1)}) fusion(f32[512,512,4]{1,0,2:T(8,128)S(1)} %fusion.11, pred[512,512]{0,1:T(8,128)(4,1)S(1)} %iota_compare_fusion.4), kind=kOutput, calls=%fused_computation.76 | output fusion | flops 6291967 | bytes 8658944 | tf_op jit(solution)/shard_map/sub | solution.py:661
  143.4 0.6 fusion.8
  143.9 0.1 reshape.262
  144.1 0.3 copy.37.ctx_ref
  144.4 0.4 fusion.9
  144.9 58.8 %shard_map.122 = (bf16[4,128,512]{2,1,0:T(8,128)(2,1)S(1)}, bf16[8,96,128]{2,1,0:T(8,128)(2,1)S(1)}, s32[8,8,128]{2,1,0:T(8,128)S(1)}) custom-call(bf16[4,128,512]{2,1,0:T(8,128)(2,1)S(1)} %copy.37.ctx_ref, bf16[4,128,512]{2,1,0:T(8,128)(2,1)S(1)} %bitcast.62, bf16[4,512,2048]{2,1,0:T(8,128)(2,1)} %bitcast.70, bf16[8,96,128]{2,1,0:T(8,128)(2,1)S(1)} %bitcast.63, ...), custom_call_target="tpu_custom_call" | custom-call | flops 4294967296 | bytes 10485760 | tf_op jit(solution)/shard_map/pallas_call | solution.py:570
  203.7 0.8 reshape.259
  204.5 0.6 reshape_squeeze.3
  205.1 0.8 copy.46
  (24 shorter events, 0.4 us)
Async XLA Ops:
  4.4 1.0 copy-start
  5.4 127.2 %copy-start.6 = (s32[1,32]{1,0:T(1,128)S(1)}, s32[1,32]{1,0:T(1,128)}, u32[]{:S(2)}) copy-start(s32[1,32]{1,0:T(1,128)} %param.17) | copy-start | bytes 388
  5.4 127.2 %copy-start.3 = (s32[1,32,1]{1,2,0:T(1,128)S(1)}, s32[1,32,1]{1,2,0:T(1,128)}, u32[]{:S(2)}) copy-start(s32[1,32,1]{1,2,0:T(1,128)} %param.18) | copy-start | bytes 388
  128.5 9.6 %collective-permute-start = (bf16[512,128]{1,0:T(8,128)(2,1)}, bf16[512,128]{1,0:T(8,128)(2,1)S(1)}, u32[]{:S(2)}, u32[]{:S(2)}) collective-permute-start(bf16[512,128]{1,0:T(8,128)(2,1)} %convert_element_type.35), channel_id=1, source_target_pairs={{0,1},{1,0},{2,3},{3,2},{4,5},{5,4},{6,7},{7,6},{8,9},{9,8},{10,11... | collective-permute-start | bytes 393224 | tf_op jit(solution)/shard_map/ppermute | solution.py:622
  133.0 0.5 copy-start.4
  133.8 0.7 copy-start.5
  136.0 2.0 copy-start.2
  143.4 1.5 copy-start.1

commit v3 on v1

v3 whole, which is shorter than its diff:
```python
import jax
import jax.numpy as jnp
from jax import lax
from jax.experimental import pallas as pl
from jax.experimental.pallas import tpu as pltpu
from jax.sharding import PartitionSpec as P

HD = 128
PAGE = 16
EPS = 1e-05
F32 = jnp.float32
BF16 = jnp.bfloat16
MESH = pl.DeviceIdType.MESH
VMEM = pltpu.VMEM

TOK = 512
COLS = 512
KCOLS = 64
HEADS = COLS // HD
NH = 2
RH = TOK // NH
NU = 2 * NH
NK = 2 * NU
LAG = 2
PIECES = 4
PR = 128 // PIECES
WO_Z = 1
WO_X = 3
NT = 4
RT = TOK // NT
HT = RT // 2


def layer_kernel(
    tok_ref, gain_ref, wq_hbm, wk_ref, wv_ref, wo_hbm, cos_ref, sin_ref,
    shared_ref, owner_ref, page_id_ref,
    mixed_ref, pool_ref, pool_ids_ref,
    sq, blocks, own, wq_v, wkv_v, acc_q, acc_kv, got_q, got_kv,
    heads, keys, values, kv_own, kv_other, pages, ids,
    ctx, wo, opp_out, opp_in, near_out, near_in, near_part, own_part,
    w_sem, d_send, d_recv, up_send, up_recv, dn_send, dn_recv,
    yp_send, yp_recv, ym_send, ym_recv, fw_send, fw_recv, x_send, x_recv,
    sy_send, sy_recv, sz_send, sz_recv,
    wz_send, wz_recv, wx_send, wx_recv, wd_send, wd_recv, wl_sem,
    kv_send, kv_recv, cu_send, cu_recv, cd_send, cd_recv,
    a_send, a_recv, b_send, b_recv, p_send, p_recv, i_send, i_recv,
):
    core = lax.axis_index("side")
    grp = lax.axis_index("grp")
    tp = lax.axis_index("tp")
    x = grp // 2
    z_hi = lax.rem(grp, 2)
    z = tp // 4
    y = lax.rem(tp, 4)
    m = jnp.where(core == 0, z, 3 - z)
    home = z // 2 == core
    own_zz = lax.rem(z, 2)

    weights = pltpu.make_async_copy(wq_hbm, wq_v, w_sem)
    weights.start()

    z_near = [{"tp": lax.rem(z + d, 4) * 4 + y} for d in (1, 2, 3)]
    y_near = [{"tp": z * 4 + lax.rem(y + d, 4)} for d in (1, 2, 3)]
    x_near = [{"grp": lax.rem(x + d, 4) * 2 + z_hi} for d in (1, 2, 3)]
    owners = [{"side": 1 - core, "grp": jnp.int32(o)} for o in range(8)]
    sibling = {"side": 1 - core}
    barrier = pltpu.get_barrier_semaphore()
    near = z_near + y_near + x_near + owners
    for one in near:
        pl.semaphore_signal(barrier, inc=1, device_id=one, device_id_type=MESH)

    for h in range(NH):
        own[h] = (
            tok_ref[h * RH:(h + 1) * RH, :].astype(F32) * gain_ref[...].astype(F32)
        ).astype(BF16)

    def remote(src, dst, send, recv, to):
        return pltpu.make_async_remote_copy(
            src_ref=src, dst_ref=dst, send_sem=send, recv_sem=recv,
            device_id=to, device_id_type=MESH)

    def same(ref, send, recv, to):
        return remote(ref, ref, send, recv, to)

    def to_root(h):
        return remote(own.at[h], blocks.at[own_zz, y, core, h], d_send.at[h], d_recv.at[h], sibling)

    pl.semaphore_wait(barrier, len(near))

    @pl.when(jnp.logical_not(home))
    def _():
        for h in range(NH):
            to_root(h).start()

    @pl.when(home)
    def _():
        for h in range(NH):
            blocks[own_zz, y, core, h] = own[h]

    up = {"tp": jnp.where(core == 0, lax.rem(z + 1, 4), lax.rem(z + 3, 4)) * 4 + y}
    down = {"tp": jnp.where(core == 0, lax.rem(z + 3, 4), lax.rem(z + 1, 4)) * 4 + y}
    yp = y_near[0]
    ym = y_near[2]
    y1, y2, y3 = lax.rem(y + 1, 4), lax.rem(y + 2, 4), lax.rem(y + 3, 4)

    def unit(k):
        u = k // 2
        b = 1 - lax.rem(k, 2)
        zz = jnp.where(core == 0, b, 1 - b)
        first = u == 0
        mid = u <= NH
        side = jnp.where(first, core, jnp.where(mid, 1 - core, core))
        h = jnp.where(first, 0, jnp.where(mid, u - 1, u - NH))
        return b, zz, side, h

    def line(k):
        b, zz, side, h = unit(k)
        ref = blocks.at[zz, y, side, h]

        @pl.when((m == b) & (side != core))
        def _():
            same(ref, d_send.at[h], d_recv.at[h], sibling).wait_recv()

        @pl.when(m > b)
        def _():
            same(ref, up_send.at[k], up_recv.at[k], up).wait_recv()

        @pl.when(m < b)
        def _():
            same(ref, dn_send.at[k], dn_recv.at[k], down).wait_recv()

        @pl.when((m >= b) & (m < 3))
        def _():
            same(ref, up_send.at[k], up_recv.at[k], up).start()

        @pl.when((m == 1) & (b == 1))
        def _():
            same(ref, dn_send.at[k], dn_recv.at[k], down).start()

        same(ref, yp_send.at[k], yp_recv.at[k], yp).start()
        same(ref, ym_send.at[k], ym_recv.at[k], ym).start()

    def ring(k):
        b, zz, side, h = unit(k)
        low = blocks.at[zz, y3, side, h]
        high = blocks.at[zz, y1, side, h]
        same(low, yp_send.at[k], yp_recv.at[k], yp).wait_recv()

        @pl.when(lax.rem(h, 2) == 0)
        def _():
            same(low, fw_send.at[k], fw_recv.at[k], yp).start()

        same(high, ym_send.at[k], ym_recv.at[k], ym).wait_recv()

        @pl.when(lax.rem(h, 2) == 1)
        def _():
            same(high, fw_send.at[k], fw_recv.at[k], ym).start()

    def swap_q():
        return remote(acc_q.at[1 - core], got_q, x_send.at[0], x_recv.at[0], sibling)

    def swap_kv():
        return remote(acc_kv.at[1 - core], got_kv, x_send.at[1], x_recv.at[1], sibling)

    def multiply(k):
        b, zz, side, h = unit(k)
        far = blocks.at[zz, y2, side, h]
        same(far, fw_send.at[k], fw_recv.at[k], yp).wait_recv()
        rows = pl.ds(pl.multiple_of(h * RH, RH), RH)
        total_q = acc_q[side, rows, :]
        total_kv = acc_kv[side, rows, :]
        for yy in range(4):
            block = blocks[zz, yy, side, h]
            total_q += jnp.dot(block, wq_v[zz, yy], preferred_element_type=F32)
            total_kv += lax.dot_general(
                block, wkv_v[zz, yy], (((1,), (1,)), ((), ())), preferred_element_type=F32)
        acc_q[side, rows, :] = total_q
        acc_kv[side, rows, :] = total_kv

        @pl.when(k == 2 * NH + 1)
        def _():
            swap_kv().start()
            swap_q().start()

    def sum_y(d):
        return remote(sq.at[0], sq.at[d], sy_send.at[d - 1], sy_recv.at[d - 1], y_near[d - 1])

    def sum_z(d):
        return remote(sq.at[4], sq.at[4 + d], sz_send.at[d - 1], sz_recv.at[d - 1], z_near[d - 1])

    def piece(zs, xx, j):
        return wo.at[zs, xx, pl.ds(pl.multiple_of(j * PR, PR), PR), :]

    def wo_line(zz, j):
        return remote(
            wo_hbm.at[x, pl.ds(pl.multiple_of(j * PR, PR), PR), zz * 2048:(zz + 1) * 2048],
            piece(z, x, j), wz_send.at[zz, j], wz_recv.at[z, j],
            {"tp": (2 * core + zz) * 4 + y})

    def wo_landed(d, j):
        zs = lax.rem(z + d, 4)
        return same(piece(zs, x, j), wz_send.at[0, j], wz_recv.at[zs, j], z_near[d - 1])

    def wo_row(d, e, j):
        return same(piece(lax.rem(z + d, 4), x, j), wx_send.at[d - 1, e - 1, j],
                    wx_recv.at[d - 1, e - 1, j], x_near[e - 1])

    own_cols = pl.ds(pl.multiple_of(own_zz * 2048, 2048), 2048)

    def wo_local():
        return pltpu.make_async_copy(wo_hbm.at[:, :, own_cols], wo.at[z], wl_sem)

    def wo_cross(d):
        here = wo.at[lax.rem(z + d, 4)]
        return remote(wo_hbm.at[:, :, own_cols] if d == 0 else here, here,
                      wd_send.at[d], wd_recv.at[d], sibling)

    def redistribute(k):
        @pl.when((k >= WO_Z) & (k < WO_Z + PIECES))
        def _():
            for zz in range(2):
                @pl.when(2 * core + zz != z)
                def _():
                    wo_line(zz, k - WO_Z).start()

        @pl.when(home & (k == WO_Z))
        def _():
            wo_local().start()
            wo_cross(0).start()

        @pl.when(home & (k >= WO_X) & (k < WO_X + PIECES))
        def _():
            for d in (1, 2, 3):
                wo_landed(d, k - WO_X).wait_recv()
                for e in (1, 2, 3):
                    wo_row(d, e, k - WO_X).start()

    xf = tok_ref[...].astype(F32)
    sq[0] = lax.dot_general(
        jnp.ones((8, COLS), F32), xf * xf, (((1,), (1,)), ((), ())),
        precision=lax.Precision.HIGHEST, preferred_element_type=F32,
    )
    for d in (1, 2, 3):
        sum_y(d).start()
    acc_q[...] = jnp.zeros_like(acc_q)
    acc_kv[...] = jnp.zeros_like(acc_kv)
    for zz in range(2):
        for yy in range(4):
            cols = slice((zz * 4 + yy) * COLS, (zz * 4 + yy + 1) * COLS)
            wkv_v[zz, yy, :KCOLS, :] = wk_ref[:, cols]
            wkv_v[zz, yy, KCOLS:, :] = wv_ref[:, cols]
    weights.wait()

    def step(k, carry):
        @pl.when(k < NK)
        def _():
            line(k)

        @pl.when((k >= LAG) & (k < NK + LAG))
        def _():
            ring(k - LAG)

        @pl.when(k >= LAG + 1)
        def _():
            multiply(k - LAG - 1)

        redistribute(k)

        @pl.when(k == 3)
        def _():
            for d in (1, 2, 3):
                sum_y(d).wait_recv()
            sq[4] = sq[0] + sq[1] + sq[2] + sq[3]
            for d in (1, 2, 3):
                sum_z(d).start()
        return carry

    lax.fori_loop(0, NK + LAG + 1, step, 0)

    for d in (1, 2, 3):
        sum_z(d).wait_recv()
    total = (sq[4] + sq[5] + sq[6] + sq[7]).T[:, :1]
    scale = lax.rsqrt(total * (1.0 / 8192.0) + EPS)
    upper = lax.rem(y, 2) == 1
    swap_kv().wait()
    mine = (acc_kv[core] + got_kv[...]) * scale
    kv_own[...] = mine.astype(BF16)
    trade = remote(kv_own, kv_other, kv_send, kv_recv, {"tp": z * 4 + y + 1 - 2 * lax.rem(y, 2)})
    trade.start()

    @pl.when(home)
    def _():
        for d in (1, 2, 3):
            for j in range(PIECES):
                for e in (1, 2, 3):
                    wo_row(d, e, j).wait_recv()
            wo_cross(d).start()

    cosine = cos_ref[...]
    sine = sin_ref[...]
    swap_q().wait()
    q_all = (acc_q[core] + got_q[...]) * scale
    for h in range(HEADS):
        head = q_all[:, h * HD:(h + 1) * HD]
        heads[h] = (head * cosine + pltpu.roll(head, HD // 2, 1) * sine).astype(BF16)
    trade.wait()
    theirs = kv_other[...].astype(F32)
    low = jnp.where(upper, theirs, mine)
    high = jnp.where(upper, mine, theirs)
    left = lax.broadcasted_iota(jnp.int32, (TOK, HD), 1) < KCOLS
    k_full = jnp.where(left, low, pltpu.roll(high, KCOLS, 1))
    v_full = jnp.where(left, pltpu.roll(low, KCOLS, 1), high)
    k_full = k_full * cosine + pltpu.roll(k_full, HD // 2, 1) * sine
    keys[...] = k_full.astype(BF16)
    values[...] = v_full.astype(BF16)
    kv_own[...] = jnp.where(
        left,
        jnp.where(upper, pltpu.roll(k_full, KCOLS, 1), k_full),
        jnp.where(upper, v_full, pltpu.roll(v_full, KCOLS, 1)),
    ).astype(BF16)

    climb_to = z_near[0]
    descend_to = z_near[2]

    def climb(zs, t):
        return same(ctx.at[zs, t], cu_send.at[zs, t], cu_recv.at[zs, t], climb_to)

    def descend(zs, t):
        return same(ctx.at[zs, t], cd_send.at[zs, t], cd_recv.at[zs, t], descend_to)

    def attend(t):
        query = heads[:, pl.ds(pl.multiple_of(t * RT, RT), RT), :].reshape(HEADS * RT, HD)
        scores = lax.dot_general(
            query, keys[...], (((1,), (1,)), ((), ())), preferred_element_type=F32
        ) / jnp.sqrt(F32(HD))
        shape = (HEADS * RT, TOK)
        place = t * RT + lax.rem(lax.broadcasted_iota(jnp.int32, shape, 0), RT)
        scores = jnp.where(lax.broadcasted_iota(jnp.int32, shape, 1) <= place, scores, -1e30)
        weight = jnp.exp(scores - jnp.max(scores, axis=-1, keepdims=True))
        share = weight / jnp.sum(weight, axis=-1, keepdims=True)
        out = jnp.dot(share.astype(BF16), values[...], preferred_element_type=F32).astype(BF16)
        for h in range(HEADS):
            ctx[z, t, :, h * HD:(h + 1) * HD] = out[h * RT:(h + 1) * RT]

        @pl.when(z < 3)
        def _():
            climb(z, t).start()

        @pl.when(z > 0)
        def _():
            descend(z, t).start()

    def page(o):
        return remote(pages.at[o], pool_ref.at[grp], p_send.at[o], p_recv.at[grp], owners[o])

    def page_id(o):
        return remote(ids.at[o], pool_ids_ref.at[grp], i_send.at[o], i_recv.at[grp], owners[o])

    def hand_over():
        live = 1.0 - shared_ref[...].astype(F32)
        owner = owner_ref[...]
        named = lax.broadcasted_iota(jnp.int32, (8, 32), 0) == owner
        onehot = jnp.where(named, live, 0.0)
        upto = (
            lax.broadcasted_iota(jnp.int32, (32, 32), 0)
            <= lax.broadcasted_iota(jnp.int32, (32, 32), 1)
        ).astype(F32)
        count = jnp.dot(onehot, upto, preferred_element_type=F32)
        rank = jnp.sum(count * onehot, axis=0, keepdims=True) - 1.0
        slot = jnp.where(live > 0.5, owner.astype(F32) * 6.0 + rank, -1.0)
        spread = (
            lax.broadcasted_iota(jnp.int32, (32, TOK), 0)
            == lax.broadcasted_iota(jnp.int32, (32, TOK), 1) // PAGE
        ).astype(F32)
        slots = jnp.dot(jnp.broadcast_to(slot, (8, 32)), spread, preferred_element_type=F32)
        inside = lax.rem(lax.broadcasted_iota(jnp.int32, (1, TOK), 1), PAGE)
        row = slots[:1] * float(PAGE) + inside.astype(F32)
        for o in range(8):
            at = (lax.broadcasted_iota(jnp.int32, (96, TOK), 0) + o * 96).astype(F32)
            picks = jnp.where(at == row, 1.0, 0.0).astype(BF16)
            pages[o] = jnp.dot(picks, kv_own[...], preferred_element_type=F32).astype(BF16)
            rank_of = lax.broadcasted_iota(jnp.int32, (8, 32), 0)
            chosen = (slot == (rank_of + o * 6).astype(F32)) & (rank_of < 6)
            found = jnp.sum(jnp.where(chosen, page_id_ref[...] + 1, 0), axis=1, keepdims=True) - 1
            ids[o] = jnp.broadcast_to(found, (8, 128))
            page(o).start()
            page_id(o).start()

    def opposite(t, way):
        return remote(opp_out.at[t, way], opp_in.at[t, way], a_send.at[t, way],
                      a_recv.at[t, way], (yp, ym)[way])

    def neighbour(t, way):
        return remote(near_out.at[t, way], near_in.at[t, way], b_send.at[t, way],
                      b_recv.at[t, way], (yp, ym)[way])

    def fetch(t):
        for d in (1, 2, 3):
            @pl.when(z - d >= 0)
            def _():
                climb(z - d, t).wait_recv()

                @pl.when(z < 3)
                def _():
                    climb(z - d, t).start()

            @pl.when(z + d <= 3)
            def _():
                descend(z + d, t).wait_recv()

                @pl.when(z > 0)
                def _():
                    descend(z + d, t).start()

    def product(t, r):
        cols = pl.ds(pl.multiple_of(lax.rem(y + r, 4) * COLS, COLS), COLS)
        total = None
        for zs in range(4):
            part = jnp.dot(
                ctx[zs, t], wo[zs, :, :, cols].reshape(COLS, COLS), preferred_element_type=F32)
            total = part if total is None else total + part
        return total

    def compute(t):
        far = product(t, 2).astype(BF16)
        for way in (0, 1):
            opp_out[t, way] = far[way * HT:(way + 1) * HT]
            opposite(t, way).start()
        near_part[t, 0] = product(t, 1)
        near_part[t, 1] = product(t, 3)
        own_part[t] = product(t, 0)

    def pass_on(t):
        for way in (0, 1):
            opposite(t, way).wait_recv()
            with_sum = slice(way * HT, (way + 1) * HT)
            without = slice((1 - way) * HT, (2 - way) * HT)
            near_out[t, way, with_sum, :] = (
                near_part[t, way, with_sum, :] + opp_in[t, way].astype(F32)
            ).astype(BF16)
            near_out[t, way, without, :] = near_part[t, way, without, :].astype(BF16)
            neighbour(t, way).start()

    def finish(t):
        neighbour(t, 0).wait_recv()
        neighbour(t, 1).wait_recv()
        total = own_part[t] + near_in[t, 0].astype(F32) + near_in[t, 1].astype(F32)
        rows = pl.ds(pl.multiple_of(t * RT, RT), RT)
        mixed_ref[rows, :] = (tok_ref[rows, :].astype(F32) + total).astype(BF16)

    attend(0)
    attend(1)
    hand_over()

    @pl.when(home)
    def _():
        wo_local().wait()

    @pl.when(jnp.logical_not(home))
    def _():
        for d in range(4):
            wo_cross(d).wait_recv()

    def out_step(t, carry):
        @pl.when(t < NT)
        def _():
            @pl.when((t >= 1) & (t < NT - 1))
            def _():
                attend(t + 1)
            fetch(t)
            compute(t)

        @pl.when((t >= 1) & (t <= NT))
        def _():
            pass_on(t - 1)

        @pl.when(t >= 2)
        def _():
            finish(t - 2)
        return carry

    lax.fori_loop(0, NT + 2, out_step, 0)

    def drain(k, carry):
        b, zz, side, h = unit(k)
        ref = blocks.at[zz, y, side, h]

        @pl.when((m >= b) & (m < 3))
        def _():
            same(ref, up_send.at[k], up_recv.at[k], up).wait_send()

        @pl.when((m == 1) & (b == 1))
        def _():
            same(ref, dn_send.at[k], dn_recv.at[k], down).wait_send()

        same(ref, yp_send.at[k], yp_recv.at[k], yp).wait_send()
        same(ref, ym_send.at[k], ym_recv.at[k], ym).wait_send()
        same(ref, fw_send.at[k], fw_recv.at[k], yp).wait_send()
        return carry

    lax.fori_loop(0, NK, drain, 0)

    def drain_out(t, carry):
        for zs in range(4):
            @pl.when((z < 3) & (zs <= z))
            def _():
                climb(zs, t).wait_send()

            @pl.when((z > 0) & (zs >= z))
            def _():
                descend(zs, t).wait_send()

        for way in (0, 1):
            opposite(t, way).wait_send()
            neighbour(t, way).wait_send()
        return carry

    lax.fori_loop(0, NT, drain_out, 0)

    @pl.when(jnp.logical_not(home))
    def _():
        for h in range(NH):
            to_root(h).wait_send()

    for d in (1, 2, 3):
        sum_y(d).wait_send()
        sum_z(d).wait_send()

    def drain_wo(j, carry):
        for zz in range(2):
            @pl.when(2 * core + zz != z)
            def _():
                wo_line(zz, j).wait_send()

        @pl.when(home)
        def _():
            for d in (1, 2, 3):
                for e in (1, 2, 3):
                    wo_row(d, e, j).wait_send()
        return carry

    lax.fori_loop(0, PIECES, drain_wo, 0)

    @pl.when(home)
    def _():
        for d in range(4):
            wo_cross(d).wait_send()

    for o in range(8):
        page(o).wait_send()
        page_id(o).wait_send()
        remote(pages.at[o], pool_ref.at[o], p_send.at[o], p_recv.at[o], owners[o]).wait_recv()
        remote(ids.at[o], pool_ids_ref.at[o], i_send.at[o], i_recv.at[o], owners[o]).wait_recv()


def layer(tokens, gain, wq, wk, wv, wo, cosine, sine, shared, owner, page_ids):
    sem = pltpu.SemaphoreType.DMA
    vm = pl.BlockSpec(memory_space=VMEM)
    hbm = pl.BlockSpec(memory_space=pl.ANY)
    return pl.pallas_call(
        layer_kernel,
        out_shape=(
            jax.ShapeDtypeStruct((TOK, COLS), BF16),
            jax.ShapeDtypeStruct((8, 96, 128), BF16),
            jax.ShapeDtypeStruct((8, 8, 128), jnp.int32),
        ),
        in_specs=[vm, vm, hbm, vm, vm, hbm, vm, vm, vm, vm, vm],
        out_specs=(vm, vm, vm),
        scratch_shapes=[
            VMEM((8, 8, TOK), F32),
            VMEM((2, 4, 2, NH, RH, COLS), BF16),
            VMEM((NH, RH, COLS), BF16),
            VMEM((2, 4, COLS, COLS), BF16),
            VMEM((2, 4, 2 * KCOLS, COLS), BF16),
            VMEM((2, TOK, COLS), F32),
            VMEM((2, TOK, 2 * KCOLS), F32),
            VMEM((TOK, COLS), F32),
            VMEM((TOK, 2 * KCOLS), F32),
            VMEM((HEADS, TOK, HD), BF16),
            VMEM((TOK, HD), BF16),
            VMEM((TOK, HD), BF16),
            VMEM((TOK, HD), BF16),
            VMEM((TOK, HD), BF16),
            VMEM((8, 96, 128), BF16),
            VMEM((8, 8, 128), jnp.int32),
            VMEM((4, NT, RT, COLS), BF16),
            VMEM((4, 4, 128, 2048), BF16),
            VMEM((NT, 2, HT, COLS), BF16),
            VMEM((NT, 2, HT, COLS), BF16),
            VMEM((NT, 2, RT, COLS), BF16),
            VMEM((NT, 2, RT, COLS), BF16),
            VMEM((NT, 2, RT, COLS), F32),
            VMEM((NT, RT, COLS), F32),
            sem, sem((NH,)), sem((NH,)),
        ] + [sem((NK,))] * 10 + [
            sem((2,)), sem((2,)), sem((3,)), sem((3,)), sem((3,)), sem((3,)),
            sem((2, PIECES)), sem((4, PIECES)), sem((3, 3, PIECES)), sem((3, 3, PIECES)),
            sem((4,)), sem((4,)), sem, sem, sem,
            sem((4, NT)), sem((4, NT)), sem((4, NT)), sem((4, NT)),
            sem((NT, 2)), sem((NT, 2)), sem((NT, 2)), sem((NT, 2)),
            sem((8,)), sem((8,)), sem((8,)), sem((8,)),
        ],
        compiler_params=pltpu.CompilerParams(
            collective_id=0, has_side_effects=True, vmem_limit_bytes=56 * 2**20
        ),
    )(
        tokens, gain.reshape(1, COLS), wq.reshape(2, 4, COLS, COLS), wk.T, wv.T,
        wo.reshape(4, 128, 4096), cosine, sine, shared, owner, page_ids,
    )


def shards(tokens, norm_gain, wq, wk, wv, wo, span_offsets, shared_pages, page_owner, page_ids):
    half = HD // 2
    freq = jnp.exp(-jnp.log(500000.0) * (2.0 * jnp.arange(half, dtype=F32)) / HD)
    positions = span_offsets[0] + jnp.arange(TOK, dtype=jnp.int32)
    angle = positions.astype(F32)[:, None] * jnp.concatenate([freq, freq])[None, :]
    sign = jnp.where(jnp.arange(HD) < half, -1.0, 1.0).astype(F32)
    cosine = jnp.cos(angle)
    sine = jnp.sin(angle) * sign[None, :]
    mixed, pool, pool_ids = layer(
        tokens, norm_gain, wq, wk, wv, wo, cosine, sine,
        shared_pages, page_owner.reshape(1, 32), page_ids,
    )
    return mixed, pool.reshape(48, 2048), pool_ids[:, :6, 0].reshape(48)


def solution(mesh):
    in_specs = (
        P(("side", "grp"), "tp"),
        P("tp"),
        P("side", "tp"),
        P("side", "tp"),
        P("side", "tp"),
        P("tp", "side"),
        P(("side", "grp")),
        P(("side", "grp"), None),
        P(("side", "grp"), None, None),
        P(("side", "grp"), None),
    )
    out_specs = (P(("side", "grp"), "tp"), P(("side", "grp"), "tp"), P(("side", "grp")))
    return jax.shard_map(shards, mesh=mesh, in_specs=in_specs, out_specs=out_specs, check_vma=False)
```

time: 293 us -> 180 us (0.61)
  waiting for transfers between devices: 87 us -> 0 us
  Pallas kernels: 91.9 us -> 170 us
  blocking collectives: 57.8 us -> 0 us
  between operations: 15 us -> 1.3 us
  starting transfers between devices: 12.8 us -> 0 us
  matrix products: 11.7 us -> 0 us
  other arithmetic: 8.16 us -> 1.89 us
    pallas_call x1, Pallas kernels: 91.9 us -> 170 us  [layer(): pl.pallas_call(layer_kernel, out_shape=(jax.ShapeDtypeStruct((TOK, COLS),...]
    reduce_scatter x1 -> x0, waiting for transfers between devices: 74.8 us -> none  [shards(): lax.psum_scatter(terms.astype(jnp.bfloat16), 'tp', scatter_dimension=1, t...]
    psum x1 -> x0, blocking collectives: 44.9 us -> none  [shards(): squares = lax.psum(jnp.sum(xf * xf, axis=1, keepdims=True), 'tp')]
    all_to_all x1 -> x0, blocking collectives: 12.9 us -> none  [shards(): lax.all_to_all(id_buffer, 'grp', split_axis=0, concat_axis=0, tiled=True)]
    dot_general x4 -> x0, matrix products: 11.7 us -> none  [the longest x1 10.1 us: shards(): jnp.dot(context, lax.all_gather(wo, 'side', axis=1, tiled=True), preferre...]
    all_to_all x1 -> x0, starting transfers between devices: 10.6 us -> none  [shards(): lax.all_to_all(buffer, 'grp', split_axis=0, concat_axis=0, tiled=True)]
    all_to_all x1 -> x0, waiting for transfers between devices: 9.32 us -> none  [shards(): lax.all_to_all(buffer, 'grp', split_axis=0, concat_axis=0, tiled=True)]
  transfers between devices with their start and end apart: 7 -> 0, of which waited for: 4 -> 0; matrix products, arithmetic and copies ran while one was open for 5% -> 0% of each run, Pallas kernels for 31% -> 0%
where the time goes in v3:
time: 180 us; the launch traced here: 179 us
  Pallas kernels  170 us (94%)
  local copies, waits for them, and re-layouts  6.38 us (4%)
  other arithmetic  1.89 us (1%)
    pallas_call x1, Pallas kernels, layer(): pl.pallas_call(layer_kernel, out_shape=(jax.ShapeDtypeStruct((TOK, COLS),...  170 us

profile of v3, /device:TPU:2, one launch (start us, length us, event | category | flops | bytes accessed | tf_op | source)
XLA Modules:
  0.0 179.4 jit_solution(13861351849016946226)
XLA Ops:
  1.3 0.1 compare_select_fusion
  1.4 1.3 reshape.32.gain_ref
  2.6 1.8 %fusion = (f32[512,128]{1,0:T(8,128)}, f32[512,128]{1,0:T(8,128)}) fusion(f32[128]{0:T(128)S(1)} %get-tuple-element.11, f32[128]{0:T(128)S(1)} %get-tuple-element.12, f32[512]{0:T(512)S(1)} %add_convert_fusion), kind=kLoop, calls=%fused_computation.2 | loop fusion | flops 131072 | bytes 527360 | tf_op jit(solution)/shard_map/mul | solution.py:619
  4.4 169.9 %shard_map.121 = (bf16[512,512]{1,0:T(8,128)(2,1)}, bf16[8,96,128]{2,1,0:T(8,128)(2,1)}, s32[8,8,128]{2,1,0:T(8,128)}) custom-call(bf16[512,512]{1,0:T(8,128)(2,1)} %tok_ref.1, bf16[1,512]{1,0:T(2,128)(2,1)} %reshape.32.gain_ref, bf16[2,4,512,512]{3,2,1,0:T(8,128)(2,1)} %bitcast.7, bf16[64,4096]{1,0:T(8,128)(2,1)} %bitcast.9, bf16[64,4096]{1,0:T(8,128)(2,1)} %bitcast.10, ...), custom_call_target="tpu_custom_call" | custom-call | tf_op jit(solution)/shard_map/pallas_call | solution.py:560
  174.3 1.0 slice_reduce_fusion
  175.3 0.6 reshape_squeeze.3
  175.9 1.7 reshape.36
  177.6 1.9 %copy.15 = bf16[512,512]{1,0:T(8,128)(2,1)} copy(bf16[512,512]{1,0:T(8,128)(2,1)} %get-tuple-element.16) | data formatting | bytes 1048576
  (2 shorter events, 0.0 us)

commit v4 on v3

--- a/solution.py
+++ b/solution.py
@@ -17,18 +17,27 @@
 COLS = 512
 KCOLS = 64
 HEADS = COLS // HD
-NH = 2
+NH = 4
 RH = TOK // NH
 NU = 2 * NH
 NK = 2 * NU
 LAG = 2
+AHEAD = 3
 PIECES = 4
 PR = 128 // PIECES
-WO_Z = 1
-WO_X = 3
+WO_Z = 3
+WO_X = 7
+WO_D = 12
 NT = 4
 RT = TOK // NT
 HT = RT // 2
+TRADE = 4
+ATTEND = 7
+FETCH = (9, 10, 11)
+COMPUTE = 12
+PASS_ON = 14
+FINISH = 16
+STEPS = LAG + 1 + 4 * (NT - 1) + FINISH + 1
 
 
 def layer_kernel(
@@ -36,7 +45,7 @@
     shared_ref, owner_ref, page_id_ref,
     mixed_ref, pool_ref, pool_ids_ref,
     sq, blocks, own, wq_v, wkv_v, acc_q, acc_kv, got_q, got_kv,
-    heads, keys, values, kv_own, kv_other, pages, ids,
+    heads, keys, values, kv_own, kv_other, kv_page, scale, pages, ids,
     ctx, wo, opp_out, opp_in, near_out, near_in, near_part, own_part,
     w_sem, d_send, d_recv, up_send, up_recv, dn_send, dn_recv,
     yp_send, yp_recv, ym_send, ym_recv, fw_send, fw_recv, x_send, x_recv,
@@ -60,12 +69,17 @@
     weights.start()
 
     z_near = [{"tp": lax.rem(z + d, 4) * 4 + y} for d in (1, 2, 3)]
+    z_all = z_hi * 4 + z
+    z_ring = []
+    for far in (1, 2, 6, 7):
+        ahead = lax.rem(z_all + far, 8)
+        z_ring.append({"grp": x * 2 + ahead // 4, "tp": lax.rem(ahead, 4) * 4 + y})
     y_near = [{"tp": z * 4 + lax.rem(y + d, 4)} for d in (1, 2, 3)]
     x_near = [{"grp": lax.rem(x + d, 4) * 2 + z_hi} for d in (1, 2, 3)]
     owners = [{"side": 1 - core, "grp": jnp.int32(o)} for o in range(8)]
     sibling = {"side": 1 - core}
     barrier = pltpu.get_barrier_semaphore()
-    near = z_near + y_near + x_near + owners
+    near = z_near + z_ring + y_near + x_near + owners
     for one in near:
         pl.semaphore_signal(barrier, inc=1, device_id=one, device_id_type=MESH)
 
@@ -104,39 +118,48 @@
     y1, y2, y3 = lax.rem(y + 1, 4), lax.rem(y + 2, 4), lax.rem(y + 3, 4)
 
     def unit(k):
-        u = k // 2
-        b = 1 - lax.rem(k, 2)
+        b = 1 - lax.rem(k, 4) // 2
         zz = jnp.where(core == 0, b, 1 - b)
-        first = u == 0
-        mid = u <= NH
-        side = jnp.where(first, core, jnp.where(mid, 1 - core, core))
-        h = jnp.where(first, 0, jnp.where(mid, u - 1, u - NH))
+        side = jnp.where(lax.rem(k, 2) == 0, core, 1 - core)
+        h = k // 4
         return b, zz, side, h
+
+    def from_root(k, carry):
+        b, zz, side, h = unit(k)
+        ref = blocks.at[zz, y, side, h]
+
+        @pl.when(m == b)
+        def _():
+            @pl.when(side != core)
+            def _():
+                same(ref, d_send.at[h], d_recv.at[h], sibling).wait_recv()
+
+            same(ref, up_send.at[k], up_recv.at[k], up).start()
+
+            @pl.when(m == 1)
+            def _():
+                same(ref, dn_send.at[k], dn_recv.at[k], down).start()
+        return carry
 
     def line(k):
         b, zz, side, h = unit(k)
         ref = blocks.at[zz, y, side, h]
 
-        @pl.when((m == b) & (side != core))
-        def _():
-            same(ref, d_send.at[h], d_recv.at[h], sibling).wait_recv()
-
         @pl.when(m > b)
         def _():
             same(ref, up_send.at[k], up_recv.at[k], up).wait_recv()
 
+            @pl.when(m < 3)
+            def _():
+                same(ref, up_send.at[k], up_recv.at[k], up).start()
+
         @pl.when(m < b)
         def _():
             same(ref, dn_send.at[k], dn_recv.at[k], down).wait_recv()
 
-        @pl.when((m >= b) & (m < 3))
-        def _():
-            same(ref, up_send.at[k], up_recv.at[k], up).start()
-
-        @pl.when((m == 1) & (b == 1))
-        def _():
-            same(ref, dn_send.at[k], dn_recv.at[k], down).start()
-
+    def spread(k):
+        b, zz, side, h = unit(k)
+        ref = blocks.at[zz, y, side, h]
         same(ref, yp_send.at[k], yp_recv.at[k], yp).start()
         same(ref, ym_send.at[k], ym_recv.at[k], ym).start()
 
@@ -146,21 +169,26 @@
         high = blocks.at[zz, y1, side, h]
         same(low, yp_send.at[k], yp_recv.at[k], yp).wait_recv()
 
-        @pl.when(lax.rem(h, 2) == 0)
+        @pl.when(lax.rem(k, 2) == 0)
         def _():
             same(low, fw_send.at[k], fw_recv.at[k], yp).start()
 
         same(high, ym_send.at[k], ym_recv.at[k], ym).wait_recv()
 
-        @pl.when(lax.rem(h, 2) == 1)
+        @pl.when(lax.rem(k, 2) == 1)
         def _():
             same(high, fw_send.at[k], fw_recv.at[k], ym).start()
 
-    def swap_q():
-        return remote(acc_q.at[1 - core], got_q, x_send.at[0], x_recv.at[0], sibling)
-
-    def swap_kv():
-        return remote(acc_kv.at[1 - core], got_kv, x_send.at[1], x_recv.at[1], sibling)
+    def chunk(t):
+        return pl.ds(pl.multiple_of(t * RT, RT), RT)
+
+    def swap_q(t):
+        return remote(acc_q.at[1 - core, chunk(t), :], got_q.at[chunk(t), :],
+                      x_send.at[0, t], x_recv.at[0, t], sibling)
+
+    def swap_kv(t):
+        return remote(acc_kv.at[1 - core, chunk(t), :], got_kv.at[chunk(t), :],
+                      x_send.at[1, t], x_recv.at[1, t], sibling)
 
     def multiply(k):
         b, zz, side, h = unit(k)
@@ -177,10 +205,10 @@
         acc_q[side, rows, :] = total_q
         acc_kv[side, rows, :] = total_kv
 
-        @pl.when(k == 2 * NH + 1)
-        def _():
-            swap_kv().start()
-            swap_q().start()
+        @pl.when(lax.rem(k, 4) == 3)
+        def _():
+            swap_kv(h).start()
+            swap_q(h).start()
 
     def sum_y(d):
         return remote(sq.at[0], sq.at[d], sy_send.at[d - 1], sy_recv.at[d - 1], y_near[d - 1])
@@ -191,15 +219,21 @@
     def piece(zs, xx, j):
         return wo.at[zs, xx, pl.ds(pl.multiple_of(j * PR, PR), PR), :]
 
-    def wo_line(zz, j):
+    def wo_line(d, j):
+        ahead = lax.rem(z_all + (1, jnp.where(lax.rem(j, 2) == 0, 2, 6), 7)[d - 1], 8)
+        z_to = lax.rem(z + d, 4)
+        col = pl.ds(pl.multiple_of(lax.rem(z_to, 2) * 2048, 2048), 2048)
         return remote(
-            wo_hbm.at[x, pl.ds(pl.multiple_of(j * PR, PR), PR), zz * 2048:(zz + 1) * 2048],
-            piece(z, x, j), wz_send.at[zz, j], wz_recv.at[z, j],
-            {"tp": (2 * core + zz) * 4 + y})
+            wo_hbm.at[x, pl.ds(pl.multiple_of(j * PR, PR), PR), col],
+            piece(z, x, j), wz_send.at[d - 1, j], wz_recv.at[d - 1, j],
+            {"grp": x * 2 + ahead // 4, "tp": lax.rem(ahead, 4) * 4 + y})
+
+    def wo_sends(d):
+        return lax.rem(z + d, 4) // 2 == core
 
     def wo_landed(d, j):
         zs = lax.rem(z + d, 4)
-        return same(piece(zs, x, j), wz_send.at[0, j], wz_recv.at[zs, j], z_near[d - 1])
+        return same(piece(zs, x, j), wz_send.at[3 - d, j], wz_recv.at[3 - d, j], z_near[d - 1])
 
     def wo_row(d, e, j):
         return same(piece(lax.rem(z + d, 4), x, j), wx_send.at[d - 1, e - 1, j],
@@ -218,10 +252,10 @@
     def redistribute(k):
         @pl.when((k >= WO_Z) & (k < WO_Z + PIECES))
         def _():
-            for zz in range(2):
-                @pl.when(2 * core + zz != z)
+            for d in (1, 2, 3):
+                @pl.when(wo_sends(d))
                 def _():
-                    wo_line(zz, k - WO_Z).start()
+                    wo_line(d, k - WO_Z).start()
 
         @pl.when(home & (k == WO_Z))
         def _():
@@ -234,6 +268,14 @@
                 wo_landed(d, k - WO_X).wait_recv()
                 for e in (1, 2, 3):
                     wo_row(d, e, k - WO_X).start()
+
+        for d in (1, 2, 3):
+            @pl.when(home & (k == WO_D + d - 1))
+            def _():
+                for j in range(PIECES):
+                    for e in (1, 2, 3):
+                        wo_row(d, e, j).wait_recv()
+                wo_cross(d).start()
 
     xf = tok_ref[...].astype(F32)
     sq[0] = lax.dot_general(
@@ -242,6 +284,8 @@
     )
     for d in (1, 2, 3):
         sum_y(d).start()
+    lax.fori_loop(0, NK, from_root, 0)
+    line(0)
     acc_q[...] = jnp.zeros_like(acc_q)
     acc_kv[...] = jnp.zeros_like(acc_kv)
     for zz in range(2):
@@ -251,73 +295,53 @@
             wkv_v[zz, yy, KCOLS:, :] = wv_ref[:, cols]
     weights.wait()
 
-    def step(k, carry):
-        @pl.when(k < NK)
-        def _():
-            line(k)
-
-        @pl.when((k >= LAG) & (k < NK + LAG))
-        def _():
-            ring(k - LAG)
-
-        @pl.when(k >= LAG + 1)
-        def _():
-            multiply(k - LAG - 1)
-
-        redistribute(k)
-
-        @pl.when(k == 3)
+    keys[...] = jnp.zeros_like(keys)
+    values[...] = jnp.zeros_like(values)
+    upper = lax.rem(y, 2) == 1
+    left = lax.broadcasted_iota(jnp.int32, (RT, HD), 1) < KCOLS
+
+    def trade(t):
+        return remote(kv_own.at[chunk(t), :], kv_other.at[chunk(t), :], kv_send.at[t],
+                      kv_recv.at[t], {"tp": z * 4 + y + 1 - 2 * lax.rem(y, 2)})
+
+    def start_trade(t):
+        @pl.when(t == 0)
         def _():
             for d in (1, 2, 3):
-                sum_y(d).wait_recv()
-            sq[4] = sq[0] + sq[1] + sq[2] + sq[3]
-            for d in (1, 2, 3):
-                sum_z(d).start()
-        return carry
-
-    lax.fori_loop(0, NK + LAG + 1, step, 0)
-
-    for d in (1, 2, 3):
-        sum_z(d).wait_recv()
-    total = (sq[4] + sq[5] + sq[6] + sq[7]).T[:, :1]
-    scale = lax.rsqrt(total * (1.0 / 8192.0) + EPS)
-    upper = lax.rem(y, 2) == 1
-    swap_kv().wait()
-    mine = (acc_kv[core] + got_kv[...]) * scale
-    kv_own[...] = mine.astype(BF16)
-    trade = remote(kv_own, kv_other, kv_send, kv_recv, {"tp": z * 4 + y + 1 - 2 * lax.rem(y, 2)})
-    trade.start()
-
-    @pl.when(home)
-    def _():
-        for d in (1, 2, 3):
-            for j in range(PIECES):
-                for e in (1, 2, 3):
-                    wo_row(d, e, j).wait_recv()
-            wo_cross(d).start()
-
-    cosine = cos_ref[...]
-    sine = sin_ref[...]
-    swap_q().wait()
-    q_all = (acc_q[core] + got_q[...]) * scale
-    for h in range(HEADS):
-        head = q_all[:, h * HD:(h + 1) * HD]
-        heads[h] = (head * cosine + pltpu.roll(head, HD // 2, 1) * sine).astype(BF16)
-    trade.wait()
-    theirs = kv_other[...].astype(F32)
-    low = jnp.where(upper, theirs, mine)
-    high = jnp.where(upper, mine, theirs)
-    left = lax.broadcasted_iota(jnp.int32, (TOK, HD), 1) < KCOLS
-    k_full = jnp.where(left, low, pltpu.roll(high, KCOLS, 1))
-    v_full = jnp.where(left, pltpu.roll(low, KCOLS, 1), high)
-    k_full = k_full * cosine + pltpu.roll(k_full, HD // 2, 1) * sine
-    keys[...] = k_full.astype(BF16)
-    values[...] = v_full.astype(BF16)
-    kv_own[...] = jnp.where(
-        left,
-        jnp.where(upper, pltpu.roll(k_full, KCOLS, 1), k_full),
-        jnp.where(upper, v_full, pltpu.roll(v_full, KCOLS, 1)),
-    ).astype(BF16)
+                sum_z(d).wait_recv()
+            total = (sq[4] + sq[5] + sq[6] + sq[7]).T[:, :1]
+            scale[...] = jnp.broadcast_to(lax.rsqrt(total * (1.0 / 8192.0) + EPS), (TOK, HD))
+        swap_kv(t).wait()
+        swap_q(t).wait()
+        rows = chunk(t)
+        mine = (acc_kv[core, rows, :] + got_kv[rows, :]) * scale[rows, :]
+        got_kv[rows, :] = mine
+        kv_own[rows, :] = mine.astype(BF16)
+        trade(t).start()
+        cosine = cos_ref[rows, :]
+        sine = sin_ref[rows, :]
+        for h in range(HEADS):
+            cols = slice(h * HD, (h + 1) * HD)
+            head = (acc_q[core, rows, cols] + got_q[rows, cols]) * scale[rows, :]
+            heads[h, rows, :] = (head * cosine + pltpu.roll(head, HD // 2, 1) * sine).astype(BF16)
+
+    def end_trade(t):
+        trade(t).wait()
+        rows = chunk(t)
+        mine = got_kv[rows, :]
+        theirs = kv_other[rows, :].astype(F32)
+        low = jnp.where(upper, theirs, mine)
+        high = jnp.where(upper, mine, theirs)
+        k_full = jnp.where(left, low, pltpu.roll(high, KCOLS, 1))
+        v_full = jnp.where(left, pltpu.roll(low, KCOLS, 1), high)
+        k_full = k_full * cos_ref[rows, :] + pltpu.roll(k_full, HD // 2, 1) * sin_ref[rows, :]
+        keys[rows, :] = k_full.astype(BF16)
+        values[rows, :] = v_full.astype(BF16)
+        kv_page[rows, :] = jnp.where(
+            left,
+            jnp.where(upper, pltpu.roll(k_full, KCOLS, 1), k_full),
+            jnp.where(upper, v_full, pltpu.roll(v_full, KCOLS, 1)),
+        ).astype(BF16)
 
     climb_to = z_near[0]
     descend_to = z_near[2]
@@ -378,7 +402,7 @@
         for o in range(8):
             at = (lax.broadcasted_iota(jnp.int32, (96, TOK), 0) + o * 96).astype(F32)
             picks = jnp.where(at == row, 1.0, 0.0).astype(BF16)
-            pages[o] = jnp.dot(picks, kv_own[...], preferred_element_type=F32).astype(BF16)
+            pages[o] = jnp.dot(picks, kv_page[...], preferred_element_type=F32).astype(BF16)
             rank_of = lax.broadcasted_iota(jnp.int32, (8, 32), 0)
             chosen = (slot == (rank_of + o * 6).astype(F32)) & (rank_of < 6)
             found = jnp.sum(jnp.where(chosen, page_id_ref[...] + 1, 0), axis=1, keepdims=True) - 1
@@ -394,8 +418,8 @@
         return remote(near_out.at[t, way], near_in.at[t, way], b_send.at[t, way],
                       b_recv.at[t, way], (yp, ym)[way])
 
-    def fetch(t):
-        for d in (1, 2, 3):
+    def fetch(t, d):
+        if True:
             @pl.when(z - d >= 0)
             def _():
                 climb(z - d, t).wait_recv()
@@ -448,38 +472,97 @@
         rows = pl.ds(pl.multiple_of(t * RT, RT), RT)
         mixed_ref[rows, :] = (tok_ref[rows, :].astype(F32) + total).astype(BF16)
 
-    attend(0)
-    attend(1)
-    hand_over()
-
-    @pl.when(home)
-    def _():
-        wo_local().wait()
-
-    @pl.when(jnp.logical_not(home))
-    def _():
-        for d in range(4):
-            wo_cross(d).wait_recv()
-
-    def out_step(t, carry):
-        @pl.when(t < NT)
-        def _():
-            @pl.when((t >= 1) & (t < NT - 1))
-            def _():
-                attend(t + 1)
-            fetch(t)
-            compute(t)
-
-        @pl.when((t >= 1) & (t <= NT))
-        def _():
-            pass_on(t - 1)
-
-        @pl.when(t >= 2)
-        def _():
-            finish(t - 2)
+    def wo_ready():
+        @pl.when(home)
+        def _():
+            wo_local().wait()
+
+        @pl.when(jnp.logical_not(home))
+        def _():
+            for d in range(4):
+                wo_cross(d).wait_recv()
+
+    def step(k, carry):
+        @pl.when(k < NK)
+        def _():
+            spread(k)
+
+        @pl.when(k < NK - AHEAD)
+        def _():
+            line(k + AHEAD)
+
+        @pl.when((k >= LAG) & (k < NK + LAG))
+        def _():
+            ring(k - LAG)
+
+        @pl.when((k >= LAG + 1) & (k < NK + LAG + 1))
+        def _():
+            multiply(k - LAG - 1)
+
+        redistribute(k)
+
+        @pl.when(k == 3)
+        def _():
+            for d in (1, 2, 3):
+                sum_y(d).wait_recv()
+            sq[4] = sq[0] + sq[1] + sq[2] + sq[3]
+            for d in (1, 2, 3):
+                sum_z(d).start()
+
+        def at(offset):
+            since = k - (LAG + 1) - offset
+            return (since >= 0) & (since <= 4 * (NT - 1)) & (lax.rem(since, 4) == 0), since // 4
+
+        turn, t1 = at(TRADE)
+
+        @pl.when(turn)
+        def _():
+            start_trade(t1)
+
+        turn, t2 = at(ATTEND)
+
+        @pl.when(turn)
+        def _():
+            end_trade(t2)
+            attend(t2)
+
+        for d in (1, 2, 3):
+            turn, t3 = at(FETCH[d - 1])
+
+            @pl.when(turn)
+            def _():
+                fetch(t3, d)
+
+        @pl.when(k == LAG + 1 + COMPUTE)
+        def _():
+            wo_ready()
+
+        turn, t4 = at(COMPUTE)
+
+        @pl.when(turn)
+        def _():
+            compute(t4)
+
+        @pl.when(k == LAG + 2 + 4 * (NT - 1) + ATTEND)
+        def _():
+            hand_over()
+
+        turn, t5 = at(PASS_ON)
+
+        @pl.when(turn)
+        def _():
+            pass_on(t5)
+
+        turn, t6 = at(FINISH)
+
+        @pl.when(turn)
+        def _():
+            finish(t6)
         return carry
 
-    lax.fori_loop(0, NT + 2, out_step, 0)
+    for k in range(1, AHEAD):
+        line(k)
+    lax.fori_loop(0, STEPS, step, 0)
 
     def drain(k, carry):
         b, zz, side, h = unit(k)
@@ -527,10 +610,10 @@
         sum_z(d).wait_send()
 
     def drain_wo(j, carry):
-        for zz in range(2):
-            @pl.when(2 * core + zz != z)
-            def _():
-                wo_line(zz, j).wait_send()
+        for d in (1, 2, 3):
+            @pl.when(wo_sends(d))
+            def _():
+                wo_line(d, j).wait_send()
 
         @pl.when(home)
         def _():
@@ -581,6 +664,8 @@
             VMEM((TOK, HD), BF16),
             VMEM((TOK, HD), BF16),
             VMEM((TOK, HD), BF16),
+            VMEM((TOK, HD), BF16),
+            VMEM((TOK, HD), F32),
             VMEM((8, 96, 128), BF16),
             VMEM((8, 8, 128), jnp.int32),
             VMEM((4, NT, RT, COLS), BF16),
@@ -593,9 +678,9 @@
             VMEM((NT, RT, COLS), F32),
             sem, sem((NH,)), sem((NH,)),
         ] + [sem((NK,))] * 10 + [
-            sem((2,)), sem((2,)), sem((3,)), sem((3,)), sem((3,)), sem((3,)),
-            sem((2, PIECES)), sem((4, PIECES)), sem((3, 3, PIECES)), sem((3, 3, PIECES)),
-            sem((4,)), sem((4,)), sem, sem, sem,
+            sem((2, NT)), sem((2, NT)), sem((3,)), sem((3,)), sem((3,)), sem((3,)),
+            sem((3, PIECES)), sem((3, PIECES)), sem((3, 3, PIECES)), sem((3, 3, PIECES)),
+            sem((4,)), sem((4,)), sem, sem((NT,)), sem((NT,)),
             sem((4, NT)), sem((4, NT)), sem((4, NT)), sem((4, NT)),
             sem((NT, 2)), sem((NT, 2)), sem((NT, 2)), sem((NT, 2)),
             sem((8,)), sem((8,)), sem((8,)), sem((8,)),

time: 180 us -> 156 us (0.87)
  Pallas kernels: 170 us -> 146 us
    pallas_call x1, Pallas kernels: 170 us -> 146 us  [layer(): pl.pallas_call(layer_kernel, out_shape=(jax.ShapeDtypeStruct((TOK, COLS),...]
where the time goes in v4:
time: 156 us; the launch traced here: 155 us
  Pallas kernels  146 us (94%)
  local copies, waits for them, and re-layouts  6.38 us (4%)
  other arithmetic  1.89 us (1%)
    pallas_call x1, Pallas kernels, layer(): pl.pallas_call(layer_kernel, out_shape=(jax.ShapeDtypeStruct((TOK, COLS),...  146 us

profile of v4, /device:TPU:2, one launch (start us, length us, event | category | flops | bytes accessed | tf_op | source)
XLA Modules:
  0.0 155.3 jit_solution(7402133283528282169)
XLA Ops:
  1.3 0.1 compare_select_fusion
  1.4 1.3 reshape.32.gain_ref
  2.6 1.8 %fusion = (f32[512,128]{1,0:T(8,128)}, f32[512,128]{1,0:T(8,128)}) fusion(f32[128]{0:T(128)S(1)} %get-tuple-element.11, f32[128]{0:T(128)S(1)} %get-tuple-element.12, f32[512]{0:T(512)S(1)} %add_convert_fusion), kind=kLoop, calls=%fused_computation.2 | loop fusion | flops 131072 | bytes 527360 | tf_op jit(solution)/shard_map/mul | solution.py:704
  4.4 145.7 %shard_map.121 = (bf16[512,512]{1,0:T(8,128)(2,1)}, bf16[8,96,128]{2,1,0:T(8,128)(2,1)}, s32[8,8,128]{2,1,0:T(8,128)}) custom-call(bf16[512,512]{1,0:T(8,128)(2,1)} %tok_ref.1, bf16[1,512]{1,0:T(2,128)(2,1)} %reshape.32.gain_ref, bf16[2,4,512,512]{3,2,1,0:T(8,128)(2,1)} %bitcast.7, bf16[64,4096]{1,0:T(8,128)(2,1)} %bitcast.9, bf16[64,4096]{1,0:T(8,128)(2,1)} %bitcast.10, ...), custom_call_target="tpu_custom_call" | custom-call | tf_op jit(solution)/shard_map/pallas_call | solution.py:643
  150.2 1.0 slice_reduce_fusion
  151.2 0.6 reshape_squeeze.3
  151.8 1.7 %reshape.36 = bf16[48,2048]{1,0:T(8,128)(2,1)} reshape(bf16[8,96,128]{2,1,0:T(8,128)(2,1)} %get-tuple-element.7) | data formatting | bytes 393216 | tf_op jit(solution)/shard_map/reshape | solution.py:709
  153.4 1.9 %copy.15 = bf16[512,512]{1,0:T(8,128)(2,1)} copy(bf16[512,512]{1,0:T(8,128)(2,1)} %get-tuple-element.16) | data formatting | bytes 1048576
  (2 shorter events, 0.0 us)

commit v5 on v4

--- a/solution.py
+++ b/solution.py
@@ -33,10 +33,10 @@
 HT = RT // 2
 TRADE = 4
 ATTEND = 7
-FETCH = (9, 10, 11)
-COMPUTE = 12
-PASS_ON = 14
-FINISH = 16
+FETCH = (10, 12, 14)
+COMPUTE = 15
+PASS_ON = 17
+FINISH = 19
 STEPS = LAG + 1 + 4 * (NT - 1) + FINISH + 1
 
 
@@ -45,7 +45,7 @@
     shared_ref, owner_ref, page_id_ref,
     mixed_ref, pool_ref, pool_ids_ref,
     sq, blocks, own, wq_v, wkv_v, acc_q, acc_kv, got_q, got_kv,
-    heads, keys, values, kv_own, kv_other, kv_page, scale, pages, ids,
+    heads, keys, values, kv_own, kv_other, kv_page, scale, pages, ids, pool_in, ids_in,
     ctx, wo, opp_out, opp_in, near_out, near_in, near_part, own_part,
     w_sem, d_send, d_recv, up_send, up_recv, dn_send, dn_recv,
     yp_send, yp_recv, ym_send, ym_recv, fw_send, fw_recv, x_send, x_recv,
@@ -85,7 +85,7 @@
 
     for h in range(NH):
         own[h] = (
-            tok_ref[h * RH:(h + 1) * RH, :].astype(F32) * gain_ref[...].astype(F32)
+            tok_ref[h * RH:(h + 1) * RH, :].astype(F32) * gain_ref[...].astype(F32).reshape(1, COLS)
         ).astype(BF16)
 
     def remote(src, dst, send, recv, to):
@@ -375,10 +375,10 @@
             descend(z, t).start()
 
     def page(o):
-        return remote(pages.at[o], pool_ref.at[grp], p_send.at[o], p_recv.at[grp], owners[o])
+        return remote(pages.at[o], pool_in.at[grp], p_send.at[o], p_recv.at[grp], owners[o])
 
     def page_id(o):
-        return remote(ids.at[o], pool_ids_ref.at[grp], i_send.at[o], i_recv.at[grp], owners[o])
+        return remote(ids.at[o], ids_in.at[grp], i_send.at[o], i_recv.at[grp], owners[o])
 
     def hand_over():
         live = 1.0 - shared_ref[...].astype(F32)
@@ -410,6 +410,26 @@
             page(o).start()
             page_id(o).start()
 
+    def take_over():
+        for o in range(8):
+            remote(pages.at[o], pool_in.at[o], p_send.at[o], p_recv.at[o], owners[o]).wait_recv()
+            remote(ids.at[o], ids_in.at[o], i_send.at[o], i_recv.at[o], owners[o]).wait_recv()
+        token = lax.broadcasted_iota(jnp.int32, (PAGE, 48, 768), 0)
+        slot = lax.broadcasted_iota(jnp.int32, (PAGE, 48, 768), 1)
+        source = lax.broadcasted_iota(jnp.int32, (PAGE, 48, 768), 2)
+        picks = jnp.where(source == slot * PAGE + token, 1.0, 0.0).astype(BF16)
+        moved = jnp.dot(
+            picks.reshape(768, 768), pool_in[...].reshape(768, 128),
+            preferred_element_type=F32).astype(BF16)
+        for i in range(PAGE):
+            pool_ref[:, i * 128:(i + 1) * 128] = moved[i * 48:(i + 1) * 48]
+        line_ids = jnp.zeros((1, 128), jnp.int32)
+        lane = lax.broadcasted_iota(jnp.int32, (1, 128), 1)
+        for o in range(8):
+            for r in range(6):
+                line_ids = jnp.where(lane == o * 6 + r, ids_in[o, r:r + 1, :], line_ids)
+        pool_ids_ref[...] = line_ids
+
     def opposite(t, way):
         return remote(opp_out.at[t, way], opp_in.at[t, way], a_send.at[t, way],
                       a_recv.at[t, way], (yp, ym)[way])
@@ -553,6 +573,10 @@
         def _():
             pass_on(t5)
 
+        @pl.when(k == LAG + 2 + 4 * (NT - 1) + PASS_ON)
+        def _():
+            take_over()
+
         turn, t6 = at(FINISH)
 
         @pl.when(turn)
@@ -632,8 +656,6 @@
     for o in range(8):
         page(o).wait_send()
         page_id(o).wait_send()
-        remote(pages.at[o], pool_ref.at[o], p_send.at[o], p_recv.at[o], owners[o]).wait_recv()
-        remote(ids.at[o], pool_ids_ref.at[o], i_send.at[o], i_recv.at[o], owners[o]).wait_recv()
 
 
 def layer(tokens, gain, wq, wk, wv, wo, cosine, sine, shared, owner, page_ids):
@@ -644,8 +666,8 @@
         layer_kernel,
         out_shape=(
             jax.ShapeDtypeStruct((TOK, COLS), BF16),
-            jax.ShapeDtypeStruct((8, 96, 128), BF16),
-            jax.ShapeDtypeStruct((8, 8, 128), jnp.int32),
+            jax.ShapeDtypeStruct((48, 2048), BF16),
+            jax.ShapeDtypeStruct((1, 128), jnp.int32),
         ),
         in_specs=[vm, vm, hbm, vm, vm, hbm, vm, vm, vm, vm, vm],
         out_specs=(vm, vm, vm),
@@ -666,6 +688,8 @@
             VMEM((TOK, HD), BF16),
             VMEM((TOK, HD), BF16),
             VMEM((TOK, HD), F32),
+            VMEM((8, 96, 128), BF16),
+            VMEM((8, 8, 128), jnp.int32),
             VMEM((8, 96, 128), BF16),
             VMEM((8, 8, 128), jnp.int32),
             VMEM((4, NT, RT, COLS), BF16),
@@ -689,7 +713,7 @@
             collective_id=0, has_side_effects=True, vmem_limit_bytes=56 * 2**20
         ),
     )(
-        tokens, gain.reshape(1, COLS), wq.reshape(2, 4, COLS, COLS), wk.T, wv.T,
+        tokens, gain, wq.reshape(2, 4, COLS, COLS), wk.T, wv.T,
         wo.reshape(4, 128, 4096), cosine, sine, shared, owner, page_ids,
     )
 
@@ -706,7 +730,7 @@
         tokens, norm_gain, wq, wk, wv, wo, cosine, sine,
         shared_pages, page_owner.reshape(1, 32), page_ids,
     )
-    return mixed, pool.reshape(48, 2048), pool_ids[:, :6, 0].reshape(48)
+    return mixed, pool, pool_ids[0, :48]
 
 
 def solution(mesh):

time: 156 us -> 151 us (0.968)
  Pallas kernels: 146 us -> 142 us
  local copies, waits for them, and re-layouts: 6.38 us -> 4.67 us
    pallas_call x1, Pallas kernels: 146 us -> 142 us  [layer(): pl.pallas_call(layer_kernel, out_shape=(jax.ShapeDtypeStruct((TOK, COLS),...]
    reshape x2 -> x0, local copies, waits for them, and re-layouts: 2.95 us -> none  [the longest x1 1.69 us: shards(): return (mixed, pool.reshape(48, 2048), pool_ids[:, :6, 0].reshape(48))]
    unnamed x1 -> x2, local copies, waits for them, and re-layouts: 1.87 us -> 3.48 us
where the time goes in v5:
time: 151 us; the launch traced here: 150 us
  Pallas kernels  142 us (94%)
  local copies, waits for them, and re-layouts  4.67 us (3%)
  other arithmetic  1.89 us (1%)
    pallas_call x1, Pallas kernels, layer(): pl.pallas_call(layer_kernel, out_shape=(jax.ShapeDtypeStruct((TOK, COLS),...  142 us
    unnamed x2, local copies, waits for them, and re-layouts  3.48 us

profile of v5, /device:TPU:2, one launch (start us, length us, event | category | flops | bytes accessed | tf_op | source)
XLA Modules:
  0.0 149.8 jit_solution(7084164578965672738)
XLA Ops:
  1.3 0.1 compare_select_fusion
  1.4 1.8 %fusion = (f32[512,128]{1,0:T(8,128)}, f32[512,128]{1,0:T(8,128)}) fusion(f32[128]{0:T(128)S(1)} %get-tuple-element.11, f32[128]{0:T(128)S(1)} %get-tuple-element.12, f32[512]{0:T(512)S(1)} %add_convert_fusion), kind=kLoop, calls=%fused_computation.2 | loop fusion | flops 131072 | bytes 527360 | tf_op jit(solution)/shard_map/mul | solution.py:728
  3.2 142.0 %shard_map.121 = (bf16[512,512]{1,0:T(8,128)(2,1)}, bf16[48,2048]{1,0:T(8,128)(2,1)}, s32[1,128]{1,0:T(1,128)}) custom-call(bf16[512,512]{1,0:T(8,128)(2,1)} %tok_ref.1, bf16[512]{0:T(512)(128)(2,1)} %gain_ref.1, bf16[2,4,512,512]{3,2,1,0:T(8,128)(2,1)} %bitcast.9, bf16[64,4096]{1,0:T(8,128)(2,1)} %bitcast.11, bf16[64,4096]{1,0:T(8,128)(2,1)} %bitcast.12, ...), custom_call_target="tpu_custom_call" | custom-call | tf_op jit(solution)/shard_map/pallas_call | solution.py:665
  145.2 1.2 slice_bitcast_fusion
  146.4 1.9 %copy.16 = bf16[512,512]{1,0:T(8,128)(2,1)} copy(bf16[512,512]{1,0:T(8,128)(2,1)} %get-tuple-element.16) | data formatting | bytes 1048576
  148.2 1.6 %copy.17 = bf16[48,2048]{1,0:T(8,128)(2,1)} copy(bf16[48,2048]{1,0:T(8,128)(2,1)} %get-tuple-element.17) | data formatting | bytes 393216
  (2 shorter events, 0.0 us)

commit v6 on v5

--- a/solution.py
+++ b/solution.py
@@ -41,11 +41,11 @@
 
 
 def layer_kernel(
-    tok_ref, gain_ref, wq_hbm, wk_ref, wv_ref, wo_hbm, cos_ref, sin_ref,
+    tok_ref, gain_ref, wq_hbm, wk_ref, wv_ref, wo_hbm, cos_in, sin_in,
     shared_ref, owner_ref, page_id_ref,
     mixed_ref, pool_ref, pool_ids_ref,
     sq, blocks, own, wq_v, wkv_v, acc_q, acc_kv, got_q, got_kv,
-    heads, keys, values, kv_own, kv_other, kv_page, scale, pages, ids, pool_in, ids_in,
+    heads, keys, values, kv_own, kv_other, kv_page, scale, pages, ids, pool_in, ids_in, cos_ref, sin_ref,
     ctx, wo, opp_out, opp_in, near_out, near_in, near_part, own_part,
     w_sem, d_send, d_recv, up_send, up_recv, dn_send, dn_recv,
     yp_send, yp_recv, ym_send, ym_recv, fw_send, fw_recv, x_send, x_recv,
@@ -99,6 +99,27 @@
     def to_root(h):
         return remote(own.at[h], blocks.at[own_zz, y, core, h], d_send.at[h], d_recv.at[h], sibling)
 
+    xf = tok_ref[...].astype(F32)
+    sq[0] = lax.dot_general(
+        jnp.ones((8, COLS), F32), xf * xf, (((1,), (1,)), ((), ())),
+        precision=lax.Precision.HIGHEST, preferred_element_type=F32,
+    )
+    acc_q[...] = jnp.zeros_like(acc_q)
+    acc_kv[...] = jnp.zeros_like(acc_kv)
+    for zz in range(2):
+        for yy in range(4):
+            cols = slice((zz * 4 + yy) * COLS, (zz * 4 + yy + 1) * COLS)
+            wkv_v[zz, yy, :KCOLS, :] = wk_ref[:, cols]
+            wkv_v[zz, yy, KCOLS:, :] = wv_ref[:, cols]
+    keys[...] = jnp.zeros_like(keys)
+    values[...] = jnp.zeros_like(values)
+    cos_b, sin_b = cos_in[32:, :], sin_in[32:, :]
+    sign = jnp.where(lax.broadcasted_iota(jnp.int32, (PAGE, HD), 1) < HD // 2, -1.0, 1.0)
+    for a in range(TOK // PAGE):
+        cos_a, sin_a = cos_in[a:a + 1, :], sin_in[a:a + 1, :]
+        rows = slice(a * PAGE, (a + 1) * PAGE)
+        cos_ref[rows, :] = cos_a * cos_b - sin_a * sin_b
+        sin_ref[rows, :] = (sin_a * cos_b + cos_a * sin_b) * sign
     pl.semaphore_wait(barrier, len(near))
 
     @pl.when(jnp.logical_not(home))
@@ -277,26 +298,12 @@
                         wo_row(d, e, j).wait_recv()
                 wo_cross(d).start()
 
-    xf = tok_ref[...].astype(F32)
-    sq[0] = lax.dot_general(
-        jnp.ones((8, COLS), F32), xf * xf, (((1,), (1,)), ((), ())),
-        precision=lax.Precision.HIGHEST, preferred_element_type=F32,
-    )
+    lax.fori_loop(0, NK, from_root, 0)
+    line(0)
     for d in (1, 2, 3):
         sum_y(d).start()
-    lax.fori_loop(0, NK, from_root, 0)
-    line(0)
-    acc_q[...] = jnp.zeros_like(acc_q)
-    acc_kv[...] = jnp.zeros_like(acc_kv)
-    for zz in range(2):
-        for yy in range(4):
-            cols = slice((zz * 4 + yy) * COLS, (zz * 4 + yy + 1) * COLS)
-            wkv_v[zz, yy, :KCOLS, :] = wk_ref[:, cols]
-            wkv_v[zz, yy, KCOLS:, :] = wv_ref[:, cols]
     weights.wait()
 
-    keys[...] = jnp.zeros_like(keys)
-    values[...] = jnp.zeros_like(values)
     upper = lax.rem(y, 2) == 1
     left = lax.broadcasted_iota(jnp.int32, (RT, HD), 1) < KCOLS
 
@@ -692,6 +699,8 @@
             VMEM((8, 8, 128), jnp.int32),
             VMEM((8, 96, 128), BF16),
             VMEM((8, 8, 128), jnp.int32),
+            VMEM((TOK, HD), F32),
+            VMEM((TOK, HD), F32),
             VMEM((4, NT, RT, COLS), BF16),
             VMEM((4, 4, 128, 2048), BF16),
             VMEM((NT, 2, HT, COLS), BF16),
@@ -721,11 +730,12 @@
 def shards(tokens, norm_gain, wq, wk, wv, wo, span_offsets, shared_pages, page_owner, page_ids):
     half = HD // 2
     freq = jnp.exp(-jnp.log(500000.0) * (2.0 * jnp.arange(half, dtype=F32)) / HD)
-    positions = span_offsets[0] + jnp.arange(TOK, dtype=jnp.int32)
-    angle = positions.astype(F32)[:, None] * jnp.concatenate([freq, freq])[None, :]
-    sign = jnp.where(jnp.arange(HD) < half, -1.0, 1.0).astype(F32)
+    marks = jnp.concatenate(
+        [span_offsets[0] + PAGE * jnp.arange(TOK // PAGE, dtype=jnp.int32),
+         jnp.arange(PAGE, dtype=jnp.int32)])
+    angle = marks.astype(F32)[:, None] * jnp.concatenate([freq, freq])[None, :]
     cosine = jnp.cos(angle)
-    sine = jnp.sin(angle) * sign[None, :]
+    sine = jnp.sin(angle)
     mixed, pool, pool_ids = layer(
         tokens, norm_gain, wq, wk, wv, wo, cosine, sine,
         shared_pages, page_owner.reshape(1, 32), page_ids,

time: 151 us -> 149 us (0.987)
  Pallas kernels: 142 us -> 140 us
    pallas_call x1, Pallas kernels: 142 us -> 140 us  [layer(): pl.pallas_call(layer_kernel, out_shape=(jax.ShapeDtypeStruct((TOK, COLS),...]
    mul x1 -> x0, other arithmetic: 1.8 us -> none  [shards(): sine = jnp.sin(angle) * sign[None, :]]
where the time goes in v6:
time: 149 us; the launch traced here: 147 us
  Pallas kernels  140 us (94%)
  local copies, waits for them, and re-layouts  4.66 us (3%)
    pallas_call x1, Pallas kernels, layer(): pl.pallas_call(layer_kernel, out_shape=(jax.ShapeDtypeStruct((TOK, COLS),...  140 us
    unnamed x2, local copies, waits for them, and re-layouts  3.48 us

profile of v6, /device:TPU:2, one launch (start us, length us, event | category | flops | bytes accessed | tf_op | source)
XLA Modules:
  0.0 146.5 jit_solution(12444794800999285122)
XLA Ops:
  1.3 0.1 pad_maximum_fusion
  1.4 0.1 add_convert_fusion
  1.5 0.8 multiply_sine_fusion
  2.3 139.6 %shard_map.121 = (bf16[512,512]{1,0:T(8,128)(2,1)}, bf16[48,2048]{1,0:T(8,128)(2,1)}, s32[1,128]{1,0:T(1,128)}) custom-call(bf16[512,512]{1,0:T(8,128)(2,1)} %tok_ref.1, bf16[512]{0:T(512)(128)(2,1)} %gain_ref.1, bf16[2,4,512,512]{3,2,1,0:T(8,128)(2,1)} %bitcast.9, bf16[64,4096]{1,0:T(8,128)(2,1)} %bitcast.11, bf16[64,4096]{1,0:T(8,128)(2,1)} %bitcast.12, ...), custom_call_target="tpu_custom_call" | custom-call | tf_op jit(solution)/shard_map/pallas_call | solution.py:672
  141.8 1.2 slice_bitcast_fusion
  143.0 1.9 %copy.16 = bf16[512,512]{1,0:T(8,128)(2,1)} copy(bf16[512,512]{1,0:T(8,128)(2,1)} %get-tuple-element.14) | data formatting | bytes 1048576
  144.9 1.6 %copy.17 = bf16[48,2048]{1,0:T(8,128)(2,1)} copy(bf16[48,2048]{1,0:T(8,128)(2,1)} %get-tuple-element.15) | data formatting | bytes 393216
  (3 shorter events, 0.0 us)

commit v7 on v6

--- a/solution.py
+++ b/solution.py
@@ -21,13 +21,13 @@
 RH = TOK // NH
 NU = 2 * NH
 NK = 2 * NU
-LAG = 2
+LAG = 3
 AHEAD = 3
 PIECES = 4
 PR = 128 // PIECES
-WO_Z = 3
-WO_X = 7
-WO_D = 12
+WO_Z = 4
+WO_X = 8
+WO_D = 14
 NT = 4
 RT = TOK // NT
 HT = RT // 2

time: 149 us -> 152 us (1.020)
  Pallas kernels: 140 us -> 143 us
    pallas_call x1, Pallas kernels: 140 us -> 143 us  [layer(): pl.pallas_call(layer_kernel, out_shape=(jax.ShapeDtypeStruct((TOK, COLS),...]
where the time goes in v7:
time: 152 us; the launch traced here: 150 us
  Pallas kernels  143 us (94%)
  local copies, waits for them, and re-layouts  4.66 us (3%)
    pallas_call x1, Pallas kernels, layer(): pl.pallas_call(layer_kernel, out_shape=(jax.ShapeDtypeStruct((TOK, COLS),...  143 us
    unnamed x2, local copies, waits for them, and re-layouts  3.48 us

profile of v7, /device:TPU:2, one launch (start us, length us, event | category | flops | bytes accessed | tf_op | source)
XLA Modules:
  0.0 149.5 jit_solution(1275613615969533837)
XLA Ops:
  1.3 0.1 pad_maximum_fusion
  1.4 0.1 add_convert_fusion
  1.5 0.8 multiply_sine_fusion
  2.3 142.6 %shard_map.121 = (bf16[512,512]{1,0:T(8,128)(2,1)}, bf16[48,2048]{1,0:T(8,128)(2,1)}, s32[1,128]{1,0:T(1,128)}) custom-call(bf16[512,512]{1,0:T(8,128)(2,1)} %tok_ref.1, bf16[512]{0:T(512)(128)(2,1)} %gain_ref.1, bf16[2,4,512,512]{3,2,1,0:T(8,128)(2,1)} %bitcast.9, bf16[64,4096]{1,0:T(8,128)(2,1)} %bitcast.11, bf16[64,4096]{1,0:T(8,128)(2,1)} %bitcast.12, ...), custom_call_target="tpu_custom_call" | custom-call | tf_op jit(solution)/shard_map/pallas_call | solution.py:672
  144.9 1.2 slice_bitcast_fusion
  146.1 1.9 %copy.16 = bf16[512,512]{1,0:T(8,128)(2,1)} copy(bf16[512,512]{1,0:T(8,128)(2,1)} %get-tuple-element.14) | data formatting | bytes 1048576
  147.9 1.6 %copy.17 = bf16[48,2048]{1,0:T(8,128)(2,1)} copy(bf16[48,2048]{1,0:T(8,128)(2,1)} %get-tuple-element.15) | data formatting | bytes 393216
  (3 shorter events, 0.0 us)
